TPU v7x, 32 devices: a whole 2x2x4 slice. The times are simulated.
32 devices in a mesh: strip: 4 (over y, core), depth: 8 (over z, x).
Axes of the slice: x: 2, y: 2, z: 4, core: 2. Of those that a mesh axis runs over, the one named last changes fastest.
Arguments:
- warmth_before: float32 [256, 256, 1024], P('depth', 'strip'), may hold values from -6 to 6
- stratum_category: int32 [256, 256, 1024], P('depth', 'strip'), may hold values from 0 to 7
- conductance_catalogue: float32 [8], replicated, may hold values from 0.3 to 3
- pivot_matrix_reciprocal: float32 [256, 32], P('depth'), may hold values from 0 to 1, as said below
- linkage_factor: float32 [8], P('depth'), may hold values from 0 to 1, as said below
- well_position_inside: int32 [512], P('strip'), may hold values from 0 to 65535, as said below
- well_holder_sequence: int32 [512], P('strip'), may hold values from 0 to 127, as said below
- well_reach: int32 [512], P('strip'), may hold values from 64 to 256
- entering_warmth: float32 [512], P('strip'), may hold values from -4 to 4
- well_transfer_speed: float32 [512], P('strip'), may hold values from 0.0005 to 0.03
Outputs:
- new_temperature: float32 [256, 256, 1024], P('depth', 'strip')
- leaving_warmth: float32 [512], P(('strip', 'depth'))
Inputs may be any that keep to these rules, and one draw needn't show every extreme that they name: `well_position_inside`: within each strip's block of 128 entries the positions are distinct; a position counts y * 1024 + x over the strip's 64 x 1024 cells. `well_holder_sequence`: each strip's block of 128 entries is a permutation of 0 to 127. `pivot_matrix_reciprocal`: entries are positive. `linkage_factor`: entries are positive and below 1.
All inputs are finite; a program needn't handle non-finite values.
Results may differ from a plain program's by a relative error of at most 0.0003.
Values sent between devices are 32-bit elements; how exact they have to be, the bound alone decides.
No kernel may reach another device: no remote copies, remote signals or barrier semaphores. Data moves between devices by JAX's collectives and lax.ppermute only.
A program may use at most 192 MiB of HBM per device.

v0:
```python
import functools

import jax
import jax.numpy as jnp
from jax import lax
from jax.experimental import pallas as pl
from jax.experimental.pallas import tpu as pltpu
from jax.sharding import PartitionSpec as P

backward_euler_advance = 0.2
storage_volume = 2.0
flux_scale = 0.5 * backward_euler_advance
LANES = 128
ROWS = 8
EDGE_VMEM = 56 * 1024 * 1024
VMEM_LIMIT = 48 * 1024 * 1024
SOLVE_VMEM = 48 * 1024 * 1024
SMALL_VMEM = 12 * 1024 * 1024
HIGHEST = lax.Precision.HIGHEST


def select_tree(category, entries):
    values = list(entries)
    bit = 1
    while len(values) > 1:
        odd = (category & bit) != 0
        values = [
            jnp.where(odd, values[k + 1], values[k]) if k + 1 < len(values) else values[k]
            for k in range(0, len(values), 2)
        ]
        bit *= 2
    return values[0]


def split_bf16(value, pieces):
    out = []
    for k in range(pieces):
        part = value.astype(jnp.bfloat16)
        out.append(part)
        if k + 1 < pieces:
            value = value - part.astype(jnp.float32)
    return out


def edge_kernel(table, w_first, cat_first, w_last, cat_last, first, last):
    slabs, rows, span = w_first.shape
    entries = [flux_scale * table[k] for k in range(table.shape[0])]
    sub = lax.broadcasted_iota(jnp.int32, (ROWS, span), 0)

    def gathered(ref, start, row):
        value = jnp.broadcast_to(ref[start, row : row + 1, :], (ROWS, span))
        for k in range(1, ROWS):
            value = jnp.where(sub == k, ref[start + k, row : row + 1, :], value)
        return value

    for w_ref, cat_ref, row, out in ((w_first, cat_first, 0, first), (w_last, cat_last, rows - 1, last)):
        for start in range(0, slabs, ROWS):
            out[0, start : start + ROWS] = gathered(w_ref, start, row)
            out[1, start : start + ROWS] = select_tree(gathered(cat_ref, start, row), entries)


def edge_rows(w, cat, table):
    slabs, lines, span = w.shape
    top = pl.BlockSpec((slabs, ROWS, span), lambda i: (0, 0, 0))
    end = pl.BlockSpec((slabs, ROWS, span), lambda i: (0, lines // ROWS - 1, 0))
    out = pl.BlockSpec((2, slabs, span), lambda i: (0, 0, 0))
    return pl.pallas_call(
        edge_kernel,
        grid=(1,),
        in_specs=[pl.BlockSpec(memory_space=pltpu.SMEM), top, top, end, end],
        out_specs=[out, out],
        out_shape=[jax.ShapeDtypeStruct((2, slabs, span), jnp.float32)] * 2,
        compiler_params=pltpu.CompilerParams(vmem_limit_bytes=EDGE_VMEM),
        cost_estimate=pl.CostEstimate(flops=10**6, bytes_accessed=w.size, transcendentals=0),
        name="edge_rows",
    )(table, w, cat, w, cat)


def stencil_kernel(
    table,
    ends,
    w_ref,
    cat_ref,
    place,
    right_ref,
    acc,
    cells_ref,
    ws,
    cs,
    fs,
    base,
    pieces,
    shift,
    pick,
    found,
):
    step = pl.program_id(0)
    planes, lines, span = w_ref.shape
    tiles = span // LANES
    groups = lines // ROWS
    wells = place.shape[1]
    entries = [flux_scale * table[k] for k in range(table.shape[0])]
    lane = lax.broadcasted_iota(jnp.int32, (lines, LANES), 1)
    own_line = lax.broadcasted_iota(jnp.int32, (lines, wells), 0) == place[...] // span
    top, end = ROWS, ROWS + lines
    dot = functools.partial(jnp.dot, preferred_element_type=jnp.float32)

    @pl.when(step == 0)
    def _():
        acc[...] = jnp.zeros_like(acc)
        base[...] = jnp.zeros_like(base)
        pieces[...] = jnp.zeros_like(pieces)
        source = lax.broadcasted_iota(jnp.int32, shift.shape, 0) % (2 * LANES)
        target = lax.broadcasted_iota(jnp.int32, shift.shape, 1)
        shift[...] = (source == target + 1).astype(jnp.float32).astype(jnp.bfloat16)
        column = lax.broadcasted_iota(jnp.int32, (span, wells), 0)
        pick[...] = (column == place[...] % span).astype(jnp.float32).astype(jnp.bfloat16)

    def keep_face(slot, t, face):
        for n, part in enumerate(split_bf16(face, 2)):
            pieces[slot, n, t] = part

    def faces(k, slot):
        left_w = left_c = jnp.zeros((lines, LANES), jnp.float32)
        for t in range(tiles):
            cols = slice(t * LANES, (t + 1) * LANES)
            w = w_ref[k, :, cols]
            c = select_tree(cat_ref[k, :, cols], entries)
            for ref, value in ((ws, w), (cs, c)):
                ref[t, top:end] = value
                ref[t, top - 1 : top] = value[0:1]
            roll_w, roll_c = pltpu.roll(w, 1, 1), pltpu.roll(c, 1, 1)
            west_w = jnp.where(lane == 0, left_w, roll_w)
            west_c = jnp.where(lane == 0, left_c, roll_c)
            left_w, left_c = roll_w, roll_c
            face = (c + west_c) * (w - west_w)
            keep_face(slot, t, face)
            if t == tiles - 1:
                keep_face(slot, tiles, pltpu.roll(-c * w, 1, 1))
            north = (c + cs[t, top - 1 : end - 1]) * (w - ws[t, top - 1 : end - 1])
            fs[t, top:end] = north
            fs[t, end : end + 1] = jnp.zeros((1, LANES), jnp.float32)
            base[slot, t] = w - face - north + fs[t, top + 1 : end + 1]

    def well_cells(k):
        upper, lower = split_bf16(w_ref[k], 2)
        kinds = cat_ref[k].astype(jnp.float32).astype(jnp.bfloat16)
        sums = dot(jnp.concatenate([upper, lower, kinds], axis=0), pick[...])
        for n, value in enumerate((sums[:lines] + sums[lines : 2 * lines], sums[2 * lines :])):
            mine = jnp.where(own_line, value, 0.0)
            found[k, n : n + 1, :] = jnp.sum(mine, axis=0, keepdims=True)

    def finish(k, slot, on):
        z = step * planes + k
        end_first = jnp.where(on, ends[0, z], 0.0)
        end_last = jnp.where(on, ends[ends.shape[0] - 1, z], 0.0)
        parts = [
            pieces[slot, n, d : d + tiles].reshape(tiles * lines, LANES)
            for n in range(2)
            for d in range(2)
        ]
        east = dot(jnp.concatenate(parts, axis=1), shift[...])
        for t in range(tiles):
            cols = slice(t * LANES, (t + 1) * LANES)
            value = base[slot, t] + east[t * lines : (t + 1) * lines]
            right_ref[:, k, :, cols] = value.reshape(groups, ROWS, LANES)
            acc[0, :, cols] += end_first * value
            acc[1, :, cols] += end_last * value

    def two_planes(m, carry):
        k = 2 * m
        finish(jnp.maximum(k - 1, 0), 1, m > 0)
        faces(k, 0)
        well_cells(k)
        finish(k, 0, True)
        faces(k + 1, 1)
        well_cells(k + 1)
        return carry

    lax.fori_loop(0, planes // 2, two_planes, 0)
    finish(planes - 1, 1, True)
    for k in range(planes):
        for n in range(2):
            cells_ref[n, k : k + 1, :] = found[k, n : n + 1, :]


def stencil(w, cat, table, inverse, place_row):
    slabs, lines, span = w.shape
    planes, groups = 8, lines // ROWS
    wells = place_row.shape[1]
    block = pl.BlockSpec((planes, lines, span), lambda i: (i, 0, 0))
    smem = pl.BlockSpec(memory_space=pltpu.SMEM)
    shifted = pltpu.VMEM((span // LANES, lines + 2 * ROWS, LANES), jnp.float32)
    return pl.pallas_call(
        stencil_kernel,
        grid=(slabs // planes,),
        in_specs=[smem, smem, block, block, pl.BlockSpec((1, wells), lambda i: (0, 0))],
        out_specs=[
            pl.BlockSpec((groups, planes, ROWS, span), lambda i: (0, i, 0, 0)),
            pl.BlockSpec((2, lines, span), lambda i: (0, 0, 0)),
            pl.BlockSpec((2, planes, wells), lambda i: (0, i, 0)),
        ],
        out_shape=[
            jax.ShapeDtypeStruct((groups, slabs, ROWS, span), jnp.float32),
            jax.ShapeDtypeStruct((2, lines, span), jnp.float32),
            jax.ShapeDtypeStruct((2, slabs, wells), jnp.float32),
        ],
        scratch_shapes=[
            shifted,
            shifted,
            shifted,
            pltpu.VMEM((2, span // LANES, lines, LANES), jnp.float32),
            pltpu.VMEM((2, 2, span // LANES + 1, lines, LANES), jnp.bfloat16),
            pltpu.VMEM((4 * LANES, LANES), jnp.bfloat16),
            pltpu.VMEM((span, wells), jnp.bfloat16),
            pltpu.VMEM((planes, 2, wells), jnp.float32),
        ],
        compiler_params=pltpu.CompilerParams(vmem_limit_bytes=VMEM_LIMIT),
        cost_estimate=pl.CostEstimate(flops=40 * w.size, bytes_accessed=12 * w.size, transcendentals=0),
        name="stencil",
    )(table, inverse, w, cat, place_row)


META = 11
META_ROWS = 16


def payload_kernel(
    ratio,
    table,
    where_am_i,
    sums,
    first,
    last,
    before,
    after,
    inverse,
    cells,
    speed,
    reach,
    out_ref,
    flux_ref,
    source_ref,
    keep,
    force,
    paths,
):
    copies, _, share = out_ref.shape
    _, lines, span = sums.shape
    _, slabs, wells = cells.shape
    dot = functools.partial(jnp.dot, precision=HIGHEST, preferred_element_type=jnp.float32)
    ends = jnp.concatenate([inverse[0:1], inverse[slabs - 1 : slabs]], axis=0)
    meta = 2 * lines

    entries = [table[k] for k in range(table.shape[0])]
    level = lax.broadcasted_iota(jnp.int32, (slabs, wells), 0) + where_am_i[0] * slabs
    rock = cells[0]
    cond = select_tree(cells[1].astype(jnp.int32), entries)
    rate = jnp.where(level < reach[...], speed[...] * cond / (1.0 + cond), 0.0)
    keep[...] = 1.0 - rate
    force[...] = rate * rock
    ones, zeros = jnp.ones((1, wells), jnp.float32), jnp.zeros((1, wells), jnp.float32)
    ways = []
    for n, order in enumerate((range(slabs), reversed(range(slabs)))):
        scale, shift = ones, zeros
        for z in order:
            paths[n, 0, z : z + 1] = scale
            paths[n, 1, z : z + 1] = shift
            scale, shift = keep[z : z + 1] * scale, keep[z : z + 1] * shift + force[z : z + 1]
        ways.append((scale, shift))
    source_ref[0] = -storage_volume * rate * (2.0 * rock - paths[0, 1] - paths[1, 1])
    source_ref[1] = storage_volume * rate * paths[0, 0]
    source_ref[2] = storage_volume * rate * paths[1, 0]
    own_sums = [dot(ends, source_ref[n]) for n in range(3)]

    for d in range(copies):
        cols = slice(d * share, (d + 1) * share)
        for q in range(2):
            out_ref[d, q * lines : (q + 1) * lines] = sums[q, :, cols]
        out_ref[d, meta : meta + META_ROWS] = jnp.zeros((META_ROWS, share), jnp.float32)
        out_ref[d, meta : meta + 2, :slabs] = ends
        out_ref[d, meta : meta + 1, slabs : slabs + 1] = jnp.full((1, 1), ratio[0])
        rows = [ways[0][0], ways[0][1], ways[1][1]]
        rows += [own_sums[n][q : q + 1] for q in range(2) for n in range(3)]
        for n, row in enumerate(rows):
            out_ref[d, meta + 2 + n : meta + 3 + n, :wells] = row
    for own, other, line, n in ((first, before, 0, 0), (last, after, lines - 1, 1)):
        flux = (own[1] + other[1]) * (other[0] - own[0])
        flux_ref[n] = flux
        extra = dot(ends, flux)
        for d in range(copies):
            for q in range(2):
                at = q * lines + line
                out_ref[d, at : at + 1] += extra[q : q + 1, d * share : (d + 1) * share]


def payload(ratio, table, depth_index, sums, edges, inverse, cells, speed, reach, copies):
    _, lines, span = sums.shape
    _, slabs, wells = cells.shape
    share = span // copies
    smem = pl.BlockSpec(memory_space=pltpu.SMEM)
    vmem = pl.BlockSpec(memory_space=pltpu.VMEM)
    column = pltpu.VMEM((slabs, wells), jnp.float32)
    return pl.pallas_call(
        payload_kernel,
        in_specs=[smem] * 3 + [vmem] * 9,
        out_specs=[vmem] * 3,
        out_shape=[
            jax.ShapeDtypeStruct((copies, 2 * lines + META_ROWS, share), jnp.float32),
            jax.ShapeDtypeStruct((2, slabs, span), jnp.float32),
            jax.ShapeDtypeStruct((3, slabs, wells), jnp.float32),
        ],
        scratch_shapes=[column, column, pltpu.VMEM((2, 2, slabs, wells), jnp.float32)],
        compiler_params=pltpu.CompilerParams(vmem_limit_bytes=SMALL_VMEM),
        cost_estimate=pl.CostEstimate(flops=10**6, bytes_accessed=10**6, transcendentals=0),
        name="payload",
    )(ratio, table, depth_index.reshape(1), sums, *edges, inverse, cells, speed, reach)


CORNERS = ((0, 0), (0, 1), (1, 0), (1, 1))


def block_scalars(tile, slabs, shape, flipped=None):
    at = lambda row, lane: jnp.broadcast_to(tile[row : row + 1, lane : lane + 1], shape)
    corner = {(r, c): at(r, c * (slabs - 1)) for r, c in CORNERS}
    if flipped is not None:
        corner = {(r, c): jnp.where(flipped, corner[1 - r, 1 - c], corner[r, c]) for r, c in CORNERS}
    return corner, at(0, slabs)


def coupling(ratio, one, other, slabs):
    return ratio * (slabs / (slabs + 1.0)) / jnp.sqrt(one * other)


def chain(corners, couple, q=None):
    out = []
    q = jnp.zeros_like(couple[0])
    for k, corner in enumerate(corners):
        vf, vl = couple[k] * corner[0, 0], couple[k] * corner[1, 0]
        wf, wl = couple[k + 1] * corner[0, 1], couple[k + 1] * corner[1, 1]
        inverse = 1.0 / (1.0 - vf * q)
        out.append(
            dict(
                p_first=vl * q * inverse,
                p_before=vl * inverse,
                a_first=inverse,
                a_before=vf * inverse,
                a_after=wf * inverse,
                couple=couple[k],
                couple_after=couple[k + 1],
                q=q,
            )
        )
        q = wl + vl * q * wf * inverse
    return out, q


KINDS = ("p_first", "p_before", "a_first", "a_before", "a_after", "couple", "couple_after", "q")


def forward(coef, firsts, lasts):
    before = [jnp.zeros_like(firsts[0])]
    for j in range(len(firsts)):
        before.append(
            lasts[j] + coef("p_first", j) * firsts[j] + coef("p_before", j) * before[j]
        )
    return before


def backward(coef, firsts, before, after):
    blocks = len(firsts)
    above, below = [None] * blocks, [None] * blocks
    for j in reversed(range(blocks)):
        below[j] = coef("couple_after", j) * after
        here = (
            coef("a_first", j) * firsts[j]
            + coef("a_before", j) * before[j]
            + coef("a_after", j) * after
        )
        above[j] = coef("couple", j) * (before[j] + coef("q", j) * here)
        after = here
    return above, below


def half_chain(tiles, slabs, flipped, middle):
    shape = (ROWS, LANES)
    scalars = [block_scalars(tile, slabs, shape, flipped) for tile in tiles]
    couple = [jnp.zeros(shape, jnp.float32)]
    for k in range(1, len(tiles)):
        ratio = jnp.where(flipped, scalars[k - 1][1], scalars[k][1])
        couple.append(coupling(ratio, scalars[k - 1][0][1, 1], scalars[k][0][0, 0], slabs))
    couple.append(middle)
    return chain([corner for corner, _ in scalars], couple)


def meta_place(j, lines, share):
    side = share // LANES
    row = lines + j // side * META
    return slice(row, row + META), slice(j % side * LANES, (j % side + 1) * LANES)


def first_kernel(slabs, half, fl_ref, out_ref, table):
    blocks, rows, share = fl_ref.shape
    lines = (rows - META_ROWS) // 2
    flip = half[0]
    flipped = flip == 1
    block = [k + flip * (blocks - 1 - 2 * k) for k in range(blocks)]
    entries, _ = half_chain(
        [fl_ref[block[k], 2 * lines : 2 * lines + ROWS, :LANES] for k in range(blocks)],
        slabs,
        flipped,
        jnp.zeros((ROWS, LANES), jnp.float32),
    )
    for k, entry in enumerate(entries):
        for n, kind in enumerate(KINDS[:2]):
            table[k, n] = entry[kind]
    coef = lambda kind, k: table[k, KINDS.index(kind)]

    def group(g, carry):
        rows = pl.ds(pl.multiple_of(g * ROWS, ROWS), ROWS)
        outer = pl.ds(pl.multiple_of(flip * lines + g * ROWS, ROWS), ROWS)
        inner = pl.ds(pl.multiple_of((1 - flip) * lines + g * ROWS, ROWS), ROWS)
        for t in range(share // LANES):
            cols = slice(t * LANES, (t + 1) * LANES)
            before = forward(
                coef,
                [fl_ref[block[k], outer, cols] for k in range(blocks)],
                [fl_ref[block[k], inner, cols] for k in range(blocks)],
            )
            out_ref[rows, cols] = before[blocks]
        return carry

    lax.fori_loop(0, lines // ROWS, group, 0)
    out_ref[lines:, :] = jnp.zeros((out_ref.shape[0] - lines, share), jnp.float32)
    for j in range(blocks):
        rows, cols = meta_place(j, lines, share)
        out_ref[rows, cols] = fl_ref[j, 2 * lines : 2 * lines + META, :LANES]


def first_half(half, fl, slabs):
    parts, rows, share = fl.shape
    lines = (rows - META_ROWS) // 2
    vmem = pl.BlockSpec(memory_space=pltpu.VMEM)
    rows = -(-meta_place(parts - 1, lines, share)[0].stop // ROWS) * ROWS
    return pl.pallas_call(
        functools.partial(first_kernel, slabs),
        in_specs=[pl.BlockSpec(memory_space=pltpu.SMEM), vmem],
        out_specs=vmem,
        out_shape=jax.ShapeDtypeStruct((rows, share), jnp.float32),
        scratch_shapes=[pltpu.VMEM((parts, 2, ROWS, LANES), jnp.float32)],
        compiler_params=pltpu.CompilerParams(vmem_limit_bytes=SMALL_VMEM),
        cost_estimate=pl.CostEstimate(flops=4 * fl.size, bytes_accessed=5 * fl.size, transcendentals=0),
        name="reduced_in",
    )(half, fl)


def second_kernel(slabs, half, fl_ref, mine, other, uv_ref, info_ref, table):
    blocks, _, lines, share = uv_ref.shape
    flip = half[0]
    flipped = flip == 1
    block = [k + flip * (blocks - 1 - 2 * k) for k in range(blocks)]
    for j in range(blocks):
        rows, cols = meta_place(j, lines, share)
        info_ref[flip * blocks + j] = fl_ref[j, 2 * lines :, :LANES]
        info_ref[(1 - flip) * blocks + j] = jnp.zeros((META_ROWS, LANES), jnp.float32)
        info_ref[(1 - flip) * blocks + j, :META] = other[rows, cols]
    shape = (ROWS, LANES)
    above, above_ratio = block_scalars(info_ref[blocks - 1], slabs, shape)
    below, below_ratio = block_scalars(info_ref[blocks], slabs, shape)
    middle = coupling(below_ratio, above[1, 1], below[0, 0], slabs)
    tiles = lambda flip: [
        info_ref[flip * blocks + k + flip * (blocks - 1 - 2 * k)] for k in range(blocks)
    ]
    entries, q_own = half_chain(tiles(flip), slabs, flipped, middle)
    _, q_other = half_chain(tiles(1 - flip), slabs, jnp.logical_not(flipped), middle)
    for k, entry in enumerate(entries):
        for n, kind in enumerate(KINDS):
            table[k, n] = entry[kind]
    table[blocks, 0] = 1.0 / (1.0 - q_own * q_other)
    table[blocks, 1] = q_other
    coef = lambda kind, k: table[k, KINDS.index(kind)]

    def group(g, carry):
        rows = pl.ds(pl.multiple_of(g * ROWS, ROWS), ROWS)
        outside = pl.ds(pl.multiple_of(flip * lines + g * ROWS, ROWS), ROWS)
        inside = pl.ds(pl.multiple_of((1 - flip) * lines + g * ROWS, ROWS), ROWS)
        for t in range(share // LANES):
            cols = slice(t * LANES, (t + 1) * LANES)
            firsts = [fl_ref[block[k], outside, cols] for k in range(blocks)]
            lasts = [fl_ref[block[k], inside, cols] for k in range(blocks - 1)]
            before = forward(coef, firsts[:-1], lasts)
            across = table[blocks, 0] * (other[rows, cols] + table[blocks, 1] * mine[rows, cols])
            outer, inner = backward(coef, firsts, before, across)
            for k in range(blocks):
                uv_ref[block[k], flip, rows, cols] = outer[k]
                uv_ref[block[k], 1 - flip, rows, cols] = inner[k]
        return carry

    lax.fori_loop(0, lines // ROWS, group, 0)


def second_half(half, fl, mine, other, slabs):
    parts, rows, share = fl.shape
    lines = (rows - META_ROWS) // 2
    vmem = pl.BlockSpec(memory_space=pltpu.VMEM)
    return pl.pallas_call(
        functools.partial(second_kernel, slabs),
        in_specs=[pl.BlockSpec(memory_space=pltpu.SMEM), vmem, vmem, vmem],
        out_specs=[vmem, vmem],
        out_shape=[
            jax.ShapeDtypeStruct((parts, 2, lines, share), jnp.float32),
            jax.ShapeDtypeStruct((2 * parts, META_ROWS, LANES), jnp.float32),
        ],
        scratch_shapes=[pltpu.VMEM((parts + 1, len(KINDS), ROWS, LANES), jnp.float32)],
        compiler_params=pltpu.CompilerParams(vmem_limit_bytes=SMALL_VMEM),
        cost_estimate=pl.CostEstimate(flops=10 * fl.size, bytes_accessed=9 * fl.size, transcendentals=0),
        name="reduced_out",
    )(half, fl, mine, other)


def extras_kernel(where_am_i, info, source, flux, inverse, inlet, holders, wells_ref, rows_ref, leaving, found):
    blocks = info.shape[0]
    slabs, wells = wells_ref.shape
    d = where_am_i[0]
    dot = functools.partial(jnp.dot, precision=HIGHEST, preferred_element_type=jnp.float32)
    row_of = lambda j, n: info[j, 2 + n : 3 + n, :wells]
    down, rise = [None] * blocks, [None] * blocks
    value = inlet[...]
    for j in range(blocks):
        down[j] = value
        value = row_of(j, 0) * value + row_of(j, 1)
    for j in reversed(range(blocks)):
        rise[j] = value
        value = row_of(j, 0) * value + row_of(j, 2)
    held = holders[...] == lax.broadcasted_iota(jnp.int32, (wells, holders.shape[1]), 0)
    leaving[...] = dot(jnp.broadcast_to(value, (ROWS, wells)), held.astype(jnp.float32))[0:1]

    ends = [
        [row_of(j, n) + row_of(j, n + 1) * down[j] + row_of(j, n + 2) * rise[j] for j in range(blocks)]
        for n in (3, 6)
    ]
    scalars = [block_scalars(info[j], slabs, (1, wells)) for j in range(blocks)]
    zero = jnp.zeros((1, wells), jnp.float32)
    couple = [zero]
    for j in range(1, blocks):
        couple.append(
            coupling(scalars[j][1], scalars[j - 1][0][1, 1], scalars[j][0][0, 0], slabs)
        )
    couple.append(zero)
    coefs, _ = chain([corner for corner, _ in scalars], couple)
    coef = lambda kind, j: coefs[j][kind]
    above, below = backward(coef, ends[0], forward(coef, *ends), zero)
    for j in range(blocks):
        for n, value in enumerate((down[j], rise[j], above[j], below[j])):
            found[j, n : n + 1] = value
    mine = found[d]
    row = lax.broadcasted_iota(jnp.int32, (slabs, wells), 0)
    own = source[0] + source[1] * mine[0:1] + source[2] * mine[1:2]
    own = own + jnp.where(row == 0, mine[2:3], 0.0) + jnp.where(row == slabs - 1, mine[3:4], 0.0)
    wells_ref[...] = dot(inverse[...], own)
    for n in range(2):
        rows_ref[n] = dot(inverse[...], flux[n])


def extras(depth_index, info, source, flux, inverse, inlet, holders):
    blocks = info.shape[0]
    _, slabs, span = flux.shape
    wells = source.shape[-1]
    vmem = pl.BlockSpec(memory_space=pltpu.VMEM)
    return pl.pallas_call(
        extras_kernel,
        in_specs=[pl.BlockSpec(memory_space=pltpu.SMEM)] + [vmem] * 6,
        out_specs=[vmem] * 3,
        out_shape=[
            jax.ShapeDtypeStruct((slabs, wells), jnp.float32),
            jax.ShapeDtypeStruct((2, slabs, span), jnp.float32),
            jax.ShapeDtypeStruct((1, holders.shape[1]), jnp.float32),
        ],
        scratch_shapes=[pltpu.VMEM((blocks, ROWS, wells), jnp.float32)],
        compiler_params=pltpu.CompilerParams(vmem_limit_bytes=SMALL_VMEM),
        cost_estimate=pl.CostEstimate(flops=10**7, bytes_accessed=10**6, transcendentals=0),
        name="extras",
    )(depth_index.reshape(1), info, source, flux, inverse, inlet, holders)


def solve_kernel(right, uv, inverse, place_row, place_column, solved_wells, outer, out, factor, pick):
    together, slabs, rows, span = right.shape
    wells = place_row.shape[1]
    step = pl.program_id(0)
    size = slabs * rows

    @pl.when(step == 0)
    def _():
        spread = (
            lax.broadcasted_iota(jnp.int32, (size, slabs), 0) // rows
            == lax.broadcasted_iota(jnp.int32, (size, slabs), 1)
        ).astype(jnp.float32).astype(jnp.bfloat16)
        spread_t = (
            lax.broadcasted_iota(jnp.int32, (slabs, size), 1) // rows
            == lax.broadcasted_iota(jnp.int32, (slabs, size), 0)
        ).astype(jnp.float32).astype(jnp.bfloat16)
        same = (
            lax.broadcasted_iota(jnp.int32, (size, size), 0) % rows
            == lax.broadcasted_iota(jnp.int32, (size, size), 1) % rows
        )
        for n, part in enumerate(split_bf16(inverse[...], 2)):
            tall = jnp.dot(spread, part, preferred_element_type=jnp.float32).astype(jnp.bfloat16)
            wide = jnp.dot(tall, spread_t, preferred_element_type=jnp.float32)
            wide = jnp.where(same, wide, 0.0).astype(jnp.bfloat16)
            if n == 0:
                factor[:, :size] = wide
                factor[:, size : 2 * size] = wide
            else:
                factor[:, 2 * size : 3 * size] = wide
        column = lax.broadcasted_iota(jnp.int32, (wells, span), 1)
        chosen = (column == place_column[...] % span).astype(jnp.float32).astype(jnp.bfloat16)
        pick[:wells] = chosen
        pick[wells:] = chosen

    tile = min(span, 256)
    for n in range(together):
        line = lax.broadcasted_iota(jnp.int32, (slabs, rows, wells), 1) + (step * together + n) * rows
        at_wells = jnp.where(line == (place_row[...] // span)[None], solved_wells[...][:, None, :], 0.0)
        at_wells = jnp.concatenate(split_bf16(at_wells.reshape(size, wells), 2), axis=1)
        factor[:, 3 * size :] = at_wells
        lines = slice(n * rows, (n + 1) * rows)
        above = jnp.concatenate([uv[d, 0, lines] for d in range(uv.shape[0])], axis=1)
        below = jnp.concatenate([uv[d, 1, lines] for d in range(uv.shape[0])], axis=1)
        for t in range(span // tile):
            cols = slice(t * tile, (t + 1) * tile)
            value = jnp.concatenate(
                [
                    right[n, 0:1, :, cols] + above[None, :, cols],
                    right[n, 1 : slabs - 1, :, cols],
                    right[n, slabs - 1 :, :, cols] + below[None, :, cols],
                ],
                axis=0,
            ).reshape(size, tile)
            upper, lower = split_bf16(value, 2)
            result = jnp.dot(
                factor[...],
                jnp.concatenate([upper, lower, upper, pick[:, cols]], axis=0),
                preferred_element_type=jnp.float32,
            )
            out[:, lines, cols] = result.reshape(slabs, rows, tile)

    for n, (when, line) in enumerate(((0, 0), (pl.num_programs(0) - 1, together * rows - 1))):

        @pl.when(step == when)
        def _():
            for z in range(slabs):
                out[z, line : line + 1, :] += outer[n, z : z + 1, :]


def solve(right, uv, inverse, place_row, solved_wells, outer):
    groups, slabs, _, span = right.shape
    wells = place_row.shape[1]
    together = 2
    lines = together * ROWS
    shares, _, _, share = uv.shape
    whole = lambda *shape: pl.BlockSpec(shape, lambda g: (0,) * len(shape))
    size = slabs * ROWS
    return pl.pallas_call(
        solve_kernel,
        grid=(groups // together,),
        in_specs=[
            pl.BlockSpec((together, slabs, ROWS, span), lambda g: (g, 0, 0, 0)),
            pl.BlockSpec((shares, 2, lines, share), lambda g: (0, 0, g, 0)),
            whole(slabs, slabs),
            whole(1, wells),
            whole(wells, 1),
            whole(slabs, wells),
            whole(*outer.shape),
        ],
        out_specs=pl.BlockSpec((slabs, lines, span), lambda g: (0, g, 0)),
        out_shape=jax.ShapeDtypeStruct((slabs, groups * ROWS, span), jnp.float32),
        scratch_shapes=[
            pltpu.VMEM((size, 3 * size + 2 * wells), jnp.bfloat16),
            pltpu.VMEM((2 * wells, span), jnp.bfloat16),
        ],
        compiler_params=pltpu.CompilerParams(vmem_limit_bytes=SOLVE_VMEM),
        cost_estimate=pl.CostEstimate(
            flops=8 * size * right.size, bytes_accessed=8 * right.size, transcendentals=0
        ),
        name="depth_solve",
    )(right, uv, inverse, place_row, place_row.reshape(wells, 1), solved_wells, outer)


def body(
    warmth_before,
    stratum_category,
    conductance_catalogue,
    pivot_matrix_reciprocal,
    linkage_factor,
    well_position_inside,
    well_holder_sequence,
    well_reach,
    entering_warmth,
    well_transfer_speed,
):
    slabs, lines, span = warmth_before.shape
    depth_index = lax.axis_index("depth")
    depth_count = lax.axis_size("depth")
    wells = well_position_inside.shape[0]
    owned = wells // depth_count
    table = conductance_catalogue

    parts = depth_count // 2
    halves = [list(range(h * parts, (h + 1) * parts)) for h in range(2)]
    half = (depth_index // parts).astype(jnp.int32).reshape(1)

    place_row = well_position_inside.reshape(1, wells)
    first, last = edge_rows(warmth_before, stratum_category, table)
    first, last, place_row = lax.optimization_barrier((first, last, place_row))
    count = lax.axis_size("strip")
    up = [(i, i + 1) for i in range(count - 1)]
    down = [(j, i) for i, j in up]
    before = lax.ppermute(last, "strip", up)
    after = lax.ppermute(first, "strip", down)
    right, sums, cells = stencil(
        warmth_before, stratum_category, table, pivot_matrix_reciprocal, place_row
    )
    fl, flux, source = payload(
        linkage_factor,
        table,
        depth_index,
        sums,
        (first, last, before, after),
        pivot_matrix_reciprocal,
        cells,
        well_transfer_speed.reshape(1, wells),
        well_reach.reshape(1, wells),
        parts,
    )
    exchange = functools.partial(
        lax.all_to_all,
        axis_name="depth",
        split_axis=0,
        concat_axis=0,
        tiled=True,
        axis_index_groups=halves,
    )
    fl_all = exchange(fl)

    mine = first_half(half, fl_all, slabs)
    other = lax.ppermute(
        mine, "depth", [(i, (i + parts) % depth_count) for i in range(depth_count)]
    )
    uv, info_all = second_half(half, fl_all, mine, other, slabs)
    uv_own = exchange(uv)

    holders = lax.dynamic_slice_in_dim(well_holder_sequence, depth_index * owned, owned)
    solved_wells, outer, leaving = extras(
        depth_index,
        info_all,
        source,
        flux,
        pivot_matrix_reciprocal,
        entering_warmth.reshape(1, wells),
        holders.reshape(1, owned),
    )
    solved = solve(right, uv_own, pivot_matrix_reciprocal, place_row, solved_wells, outer)
    return solved, leaving.reshape(owned)


def solution(mesh):
    in_specs = (
        P("depth", "strip", None),
        P("depth", "strip", None),
        P(),
        P("depth", None),
        P("depth"),
        P("strip"),
        P("strip"),
        P("strip"),
        P("strip"),
        P("strip"),
    )
    out_specs = (P("depth", "strip", None), P(("strip", "depth")))
    return jax.shard_map(body, mesh=mesh, in_specs=in_specs, out_specs=out_specs, check_vma=False)
```

profile of v0, /device:TPU:0, one launch (start us, length us, event | category | flops | bytes accessed | tf_op | source)
XLA Modules:
  0.0 79.7 jit_solution(6640451023344387413)
XLA Ops:
  0.6 0.0 copy-start
  0.6 0.0 copy-start.5
  0.7 0.0 copy-start.4
  0.7 0.0 copy-start.1
  0.7 3.3 %edge_rows.1 = (f32[2,32,1024]{2,1,0:T(8,128)}, f32[2,32,1024]{2,1,0:T(8,128)}) custom-call(f32[8]{0:T(128)} %table.5, f32[32,64,1024]{2,1,0:T(8,128)} %w_ref.1, s32[32,64,1024]{2,1,0:T(8,128)} %cat_ref.1, f32[32,64,1024]{2,1,0:T(8,128)} %w_ref.1, s32[32,64,1024]{2,1,0:T(8,128)} %cat_ref.1), custom_call_target="tpu_custom_call" | custom-call | flops 1000000 | bytes 2097152 | tf_op jit(solution)/shard_map/edge_rows/pallas_call | solution.py:67
  4.0 1.3 %collective-permute-start.1 = (f32[2,32,1024]{2,1,0:T(8,128)}, f32[2,32,1024]{2,1,0:T(8,128)S(1)}, u32[]{:S(2)}, u32[]{:S(2)}) collective-permute-start(f32[2,32,1024]{2,1,0:T(8,128)} %get-tuple-element.23.first), channel_id=1, source_target_pairs={{8,0},{16,8},{24,16},{9,1},{17,9},{25,17},{10,2},{18,10},{26,18},{... | collective-permute-start | bytes 786440 | tf_op jit(solution)/shard_map/ppermute | solution.py:719
  5.3 3.0 %collective-permute-start = (f32[2,32,1024]{2,1,0:T(8,128)}, f32[2,32,1024]{2,1,0:T(8,128)S(1)}, u32[]{:S(2)}, u32[]{:S(2)}) collective-permute-start(f32[2,32,1024]{2,1,0:T(8,128)} %get-tuple-element.24.last), channel_id=1, source_target_pairs={{0,8},{8,16},{16,24},{1,9},{9,17},{17,25},{2,10},{10,18},{18,26},{... | collective-permute-start | bytes 786440 | tf_op jit(solution)/shard_map/ppermute | solution.py:718
  9.0 0.0 copy-done.5
  9.0 0.0 copy-done.4
  9.0 0.0 copy-done.1
  9.0 0.0 copy-start.2
  9.1 0.0 copy-start.3
  9.1 0.0 copy-start.6
  9.1 0.0 copy-start.7
  9.1 0.0 copy-start.8
  9.1 23.1 %stencil.1 = (f32[8,32,8,1024]{3,2,1,0:T(8,128)}, f32[2,64,1024]{2,1,0:T(8,128)S(1)}, f32[2,32,128]{2,1,0:T(8,128)S(1)}) custom-call(f32[8]{0:T(128)S(1)} %copy-done.5, f32[32,32]{1,0:T(8,128)S(1)} %copy-done.1, f32[32,64,1024]{2,1,0:T(8,128)} %w_ref.1, s32[32,64,1024]{2,1,0:T(8,128)} %cat_ref.1, s32[1,128]{1,0:T(1,128)S(1)} %bitcast.10), custom_call_target="tpu_custom_call" | custom-call | flops 83886080 | bytes 25165824 | tf_op jit(solution)/shard_map/stencil/pallas_call | solution.py:194
  32.2 0.0 collective-permute-done.1.after
  32.2 0.0 collective-permute-done.before
  32.2 0.0 copy-done.2
  32.2 0.0 copy-done.3
  32.2 0.0 copy-done.6
  32.2 0.0 copy-done.7
  32.2 1.8 %payload.1 = (f32[4,144,256]{2,1,0:T(8,128)}, f32[2,32,1024]{2,1,0:T(8,128)S(1)}, f32[3,32,128]{2,1,0:T(8,128)S(1)}) custom-call(f32[1]{0:T(128)S(6)} %copy.13.ratio, f32[8]{0:T(128)S(1)} %copy-done.5, s32[1]{0:T(128)} %bitcast.2.where_am_i, f32[2,64,1024]{2,1,0:T(8,128)S(1)} %get-tuple-element.22.sums, f32[2,32,1024]{2,1,0:T(8,128)S(1)} %copy-done.2, ...), custom_call_target="tpu_custom_call" | custom-call | flops 1000000 | bytes 1000000 | tf_op jit(solution)/shard_map/payload/pallas_call | solution.py:304
  34.1 5.2 %all-to-all-start = ((f32[4,144,256]{2,1,0:T(8,128)}), f32[4,144,256]{2,1,0:T(8,128)S(1)}, u32[]{:S(2)}, u32[]{:S(2)}) async-start(f32[4,144,256]{2,1,0:T(8,128)} %get-tuple-element.26), calls=%async_computation | async-start | bytes 1179648 | tf_op jit(solution)/shard_map/all_to_all | solution.py:743
  39.3 10.0 %all-to-all-done.fl_ref = f32[4,144,256]{2,1,0:T(8,128)S(1)} async-done(((f32[4,144,256]{2,1,0:T(8,128)}), f32[4,144,256]{2,1,0:T(8,128)S(1)}, u32[]{:S(2)}, u32[]{:S(2)}) %all-to-all-start) | async-done | bytes 589856 | tf_op jit(solution)/shard_map/all_to_all | solution.py:743
  49.3 0.3 reduced_in.1.mine
  49.6 2.7 %collective-permute-start.2 = (f32[88,256]{1,0:T(8,128)S(1)}, f32[88,256]{1,0:T(8,128)S(1)}, u32[]{:S(2)}, u32[]{:S(2)}) collective-permute-start(f32[88,256]{1,0:T(8,128)S(1)} %reduced_in.1.mine), channel_id=1, source_target_pairs={{0,4},{1,5},{2,6},{3,7},{4,0},{5,1},{6,2},{7,3},{8,12},{9,13},{10,... | collective-permute-start | bytes 270344 | tf_op jit(solution)/shard_map/ppermute | solution.py:746
  52.3 4.8 %collective-permute-done.2.other = f32[88,256]{1,0:T(8,128)S(1)} collective-permute-done((f32[88,256]{1,0:T(8,128)S(1)}, f32[88,256]{1,0:T(8,128)S(1)}, u32[]{:S(2)}, u32[]{:S(2)}) %collective-permute-start.2) | collective-permute-done | bytes 90144 | tf_op jit(solution)/shard_map/ppermute | solution.py:746
  57.0 1.3 %reduced_out.1 = (f32[4,2,64,256]{3,2,1,0:T(8,128)}, f32[8,16,128]{2,1,0:T(8,128)S(1)}) custom-call(s32[1]{0:T(128)} %bitcast.1.half, f32[4,144,256]{2,1,0:T(8,128)S(1)} %all-to-all-done.fl_ref, f32[88,256]{1,0:T(8,128)S(1)} %reduced_in.1.mine, f32[88,256]{1,0:T(8,128)S(1)} %collective-permute-done.2.other), custom_call_target="tpu_custom_call" | custom-call | flops 1474560 | bytes 1327104 | tf_op jit(solution)/shard_map/reduced_out/pallas_call | solution.py:506
  58.3 3.5 %all-to-all-start.1 = ((f32[4,2,64,256]{3,2,1,0:T(8,128)}), f32[4,2,64,256]{3,2,1,0:T(8,128)S(1)}, u32[]{:S(2)}, u32[]{:S(2)}) async-start(f32[4,2,64,256]{3,2,1,0:T(8,128)} %get-tuple-element.27), calls=%async_computation.1 | async-start | bytes 1048576 | tf_op jit(solution)/shard_map/all_to_all | solution.py:750
  61.8 0.1 copy.12.place_column
  61.9 0.0 copy-done
  61.9 0.1 dynamic-slice_bitcast_fusion.holders
  61.9 0.0 copy-done.8
  62.0 0.8 extras.1
  62.7 7.1 %all-to-all-done.1.uv = f32[4,2,64,256]{3,2,1,0:T(8,128)S(1)} async-done(((f32[4,2,64,256]{3,2,1,0:T(8,128)}), f32[4,2,64,256]{3,2,1,0:T(8,128)S(1)}, u32[]{:S(2)}, u32[]{:S(2)}) %all-to-all-start.1) | async-done | bytes 524320 | tf_op jit(solution)/shard_map/all_to_all | solution.py:750
  69.9 9.8 %depth_solve.1 = f32[32,64,1024]{2,1,0:T(8,128)} custom-call(f32[8,32,8,1024]{3,2,1,0:T(8,128)} %get-tuple-element.21.right, f32[4,2,64,256]{3,2,1,0:T(8,128)S(1)} %all-to-all-done.1.uv, f32[32,32]{1,0:T(8,128)S(1)} %copy-done.1, s32[1,128]{1,0:T(1,128)S(1)} %bitcast.12, s32[128,1]{1,0:T(8,128)S(1)} %copy.12.place_column, ...), custom_call_target="tpu_custom_call" | custom-call | flops 4294967296 | bytes 16777216 | tf_op jit(solution)/shard_map/depth_solve/pallas_call | solution.py:663
Async XLA Ops:
  0.6 61.2 %copy-start = (s32[128]{0:T(128)S(1)}, s32[128]{0:T(128)}, u32[]{:S(2)}) copy-start(s32[128]{0:T(128)} %param.16) | copy-start | bytes 1540
  0.6 8.4 %copy-start.5 = (f32[8]{0:T(128)S(1)}, f32[8]{0:T(128)}, u32[]{:S(2)}) copy-start(f32[8]{0:T(128)} %table.5) | copy-start | bytes 100
  0.7 8.4 %copy-start.4 = (s32[128]{0:T(128)S(1)}, s32[128]{0:T(128)}, u32[]{:S(2)}) copy-start(s32[128]{0:T(128)} %param.15) | copy-start | bytes 1540
  0.7 8.4 %copy-start.1 = (f32[32,32]{1,0:T(8,128)S(1)}, f32[32,32]{1,0:T(8,128)}, u32[]{:S(2)}) copy-start(f32[32,32]{1,0:T(8,128)} %inverse.5) | copy-start | bytes 12292
  4.0 28.2 %collective-permute-start.1 = (f32[2,32,1024]{2,1,0:T(8,128)}, f32[2,32,1024]{2,1,0:T(8,128)S(1)}, u32[]{:S(2)}, u32[]{:S(2)}) collective-permute-start(f32[2,32,1024]{2,1,0:T(8,128)} %get-tuple-element.23.first), channel_id=1, source_target_pairs={{8,0},{16,8},{24,16},{9,1},{17,9},{25,17},{10,2},{18,10},{26,18},{... | collective-permute-start | bytes 786440 | tf_op jit(solution)/shard_map/ppermute | solution.py:719
  5.3 26.9 %collective-permute-start = (f32[2,32,1024]{2,1,0:T(8,128)}, f32[2,32,1024]{2,1,0:T(8,128)S(1)}, u32[]{:S(2)}, u32[]{:S(2)}) collective-permute-start(f32[2,32,1024]{2,1,0:T(8,128)} %get-tuple-element.24.last), channel_id=1, source_target_pairs={{0,8},{8,16},{16,24},{1,9},{9,17},{17,25},{2,10},{10,18},{18,26},{... | collective-permute-start | bytes 786440 | tf_op jit(solution)/shard_map/ppermute | solution.py:718
  9.0 23.2 %copy-start.2 = (f32[2,32,1024]{2,1,0:T(8,128)S(1)}, f32[2,32,1024]{2,1,0:T(8,128)}, u32[]{:S(2)}) copy-start(f32[2,32,1024]{2,1,0:T(8,128)} %get-tuple-element.23.first) | copy-start | bytes 786436
  9.1 23.2 %copy-start.3 = (f32[2,32,1024]{2,1,0:T(8,128)S(1)}, f32[2,32,1024]{2,1,0:T(8,128)}, u32[]{:S(2)}) copy-start(f32[2,32,1024]{2,1,0:T(8,128)} %get-tuple-element.24.last) | copy-start | bytes 786436
  9.1 23.2 %copy-start.6 = (f32[128]{0:T(128)S(1)}, f32[128]{0:T(128)}, u32[]{:S(2)}) copy-start(f32[128]{0:T(128)} %param.19) | copy-start | bytes 1540
  9.1 23.2 %copy-start.7 = (s32[128]{0:T(128)S(1)}, s32[128]{0:T(128)}, u32[]{:S(2)}) copy-start(s32[128]{0:T(128)} %param.17) | copy-start | bytes 1540
  9.1 52.9 %copy-start.8 = (f32[128]{0:T(128)S(1)}, f32[128]{0:T(128)}, u32[]{:S(2)}) copy-start(f32[128]{0:T(128)} %param.18) | copy-start | bytes 1540
  34.1 15.2 %all-to-all-start = ((f32[4,144,256]{2,1,0:T(8,128)}), f32[4,144,256]{2,1,0:T(8,128)S(1)}, u32[]{:S(2)}, u32[]{:S(2)}) async-start(f32[4,144,256]{2,1,0:T(8,128)} %get-tuple-element.26), calls=%async_computation | async-start | bytes 1179648 | tf_op jit(solution)/shard_map/all_to_all | solution.py:743
  49.6 7.4 %collective-permute-start.2 = (f32[88,256]{1,0:T(8,128)S(1)}, f32[88,256]{1,0:T(8,128)S(1)}, u32[]{:S(2)}, u32[]{:S(2)}) collective-permute-start(f32[88,256]{1,0:T(8,128)S(1)} %reduced_in.1.mine), channel_id=1, source_target_pairs={{0,4},{1,5},{2,6},{3,7},{4,0},{5,1},{6,2},{7,3},{8,12},{9,13},{10,... | collective-permute-start | bytes 270344 | tf_op jit(solution)/shard_map/ppermute | solution.py:746
  58.3 11.6 %all-to-all-start.1 = ((f32[4,2,64,256]{3,2,1,0:T(8,128)}), f32[4,2,64,256]{3,2,1,0:T(8,128)S(1)}, u32[]{:S(2)}, u32[]{:S(2)}) async-start(f32[4,2,64,256]{3,2,1,0:T(8,128)} %get-tuple-element.27), calls=%async_computation.1 | async-start | bytes 1048576 | tf_op jit(solution)/shard_map/all_to_all | solution.py:750
where the time goes:
time: 80 us; the launch traced here: 79.7 us
  Pallas kernels  40.4 us (50%)
  waiting for transfers between devices  21.9 us (27%)
  starting transfers between devices  15.7 us (20%)
  between operations  1.45 us (2%)
    pallas_call x1, Pallas kernels, stencil(): pl.pallas_call(stencil_kernel, grid=(slabs // planes,), in_specs=[smem, s...  23.1 us
    all_to_all x1, waiting for transfers between devices, body(): fl_all = exchange(fl)  10 us
    pallas_call x1, Pallas kernels, solve(): pl.pallas_call(solve_kernel, grid=(groups // together,), in_specs=[pl.Blo...  9.78 us
    all_to_all x1, waiting for transfers between devices, body(): uv_own = exchange(uv)  7.14 us
    all_to_all x1, starting transfers between devices, body(): fl_all = exchange(fl)  5.22 us
    ppermute x1, waiting for transfers between devices, body(): lax.ppermute(mine, 'depth', [(i, (i + parts) % depth_count) for i in rang...  4.75 us
    all_to_all x1, starting transfers between devices, body(): uv_own = exchange(uv)  3.47 us
    pallas_call x1, Pallas kernels, edge_rows(): pl.pallas_call(edge_kernel, grid=(1,), in_specs=[pl.BlockSpec(memory_spac...  3.34 us
  transfers between devices with their start and end apart: 5, of which 3 were waited for; matrix products, arithmetic and copies ran while one was open for 0% of the time, Pallas kernels for 30%

commit v1 on v0

--- a/solution.py
+++ b/solution.py
@@ -13,8 +13,8 @@
 LANES = 128
 ROWS = 8
 EDGE_VMEM = 56 * 1024 * 1024
-VMEM_LIMIT = 48 * 1024 * 1024
-SOLVE_VMEM = 48 * 1024 * 1024
+VMEM_LIMIT = 40 * 1024 * 1024
+SOLVE_VMEM = 24 * 1024 * 1024
 SMALL_VMEM = 12 * 1024 * 1024
 HIGHEST = lax.Precision.HIGHEST
 
@@ -238,14 +238,12 @@
     cells,
     speed,
     reach,
-    out_ref,
-    flux_ref,
-    source_ref,
-    keep,
-    force,
-    paths,
+    *refs,
 ):
-    copies, _, share = out_ref.shape
+    out_refs, (flux_ref, source_ref, keep, force, paths, totals) = refs[:-6], refs[-6:]
+    copies = len(out_refs)
+    share = out_refs[0].shape[1]
+    mine = where_am_i[0] & (copies - 1)
     _, lines, span = sums.shape
     _, slabs, wells = cells.shape
     dot = functools.partial(jnp.dot, precision=HIGHEST, preferred_element_type=jnp.float32)
@@ -273,28 +271,29 @@
     source_ref[2] = storage_volume * rate * paths[1, 0]
     own_sums = [dot(ends, source_ref[n]) for n in range(3)]
 
-    for d in range(copies):
-        cols = slice(d * share, (d + 1) * share)
-        for q in range(2):
-            out_ref[d, q * lines : (q + 1) * lines] = sums[q, :, cols]
-        out_ref[d, meta : meta + META_ROWS] = jnp.zeros((META_ROWS, share), jnp.float32)
-        out_ref[d, meta : meta + 2, :slabs] = ends
-        out_ref[d, meta : meta + 1, slabs : slabs + 1] = jnp.full((1, 1), ratio[0])
-        rows = [ways[0][0], ways[0][1], ways[1][1]]
-        rows += [own_sums[n][q : q + 1] for q in range(2) for n in range(3)]
-        for n, row in enumerate(rows):
-            out_ref[d, meta + 2 + n : meta + 3 + n, :wells] = row
+    rows = [ways[0][0], ways[0][1], ways[1][1]]
+    rows += [own_sums[n][q : q + 1] for q in range(2) for n in range(3)]
+    extras = []
     for own, other, line, n in ((first, before, 0, 0), (last, after, lines - 1, 1)):
         flux = (own[1] + other[1]) * (other[0] - own[0])
         flux_ref[n] = flux
-        extra = dot(ends, flux)
-        for d in range(copies):
-            for q in range(2):
-                at = q * lines + line
-                out_ref[d, at : at + 1] += extra[q : q + 1, d * share : (d + 1) * share]
-
-
-def payload(ratio, table, depth_index, sums, edges, inverse, cells, speed, reach, copies):
+        extras.append((line, dot(ends, flux)))
+    totals[...] = sums[...]
+    for line, extra in extras:
+        for q in range(2):
+            totals[q, line : line + 1, :] += extra[q : q + 1]
+    for m, out_ref in enumerate(out_refs):
+        cols = pl.ds(pl.multiple_of((mine ^ m) * share, share), share)
+        for q in range(2):
+            out_ref[q * lines : (q + 1) * lines] = totals[q, :, cols]
+        out_ref[meta : meta + META_ROWS] = jnp.zeros((META_ROWS, share), jnp.float32)
+        out_ref[meta : meta + 2, :slabs] = ends
+        out_ref[meta : meta + 1, slabs : slabs + 1] = jnp.full((1, 1), ratio[0])
+        for n, row in enumerate(rows):
+            out_ref[meta + 2 + n : meta + 3 + n, :wells] = row
+
+
+def payload(ratio, table, where, sums, edges, inverse, cells, speed, reach, copies):
     _, lines, span = sums.shape
     _, slabs, wells = cells.shape
     share = span // copies
@@ -304,17 +303,22 @@
     return pl.pallas_call(
         payload_kernel,
         in_specs=[smem] * 3 + [vmem] * 9,
-        out_specs=[vmem] * 3,
-        out_shape=[
-            jax.ShapeDtypeStruct((copies, 2 * lines + META_ROWS, share), jnp.float32),
+        out_specs=[vmem] * (copies + 2),
+        out_shape=[jax.ShapeDtypeStruct((2 * lines + META_ROWS, share), jnp.float32)] * copies
+        + [
             jax.ShapeDtypeStruct((2, slabs, span), jnp.float32),
             jax.ShapeDtypeStruct((3, slabs, wells), jnp.float32),
         ],
-        scratch_shapes=[column, column, pltpu.VMEM((2, 2, slabs, wells), jnp.float32)],
+        scratch_shapes=[
+            column,
+            column,
+            pltpu.VMEM((2, 2, slabs, wells), jnp.float32),
+            pltpu.VMEM((2, lines, span), jnp.float32),
+        ],
         compiler_params=pltpu.CompilerParams(vmem_limit_bytes=SMALL_VMEM),
         cost_estimate=pl.CostEstimate(flops=10**6, bytes_accessed=10**6, transcendentals=0),
         name="payload",
-    )(ratio, table, depth_index.reshape(1), sums, *edges, inverse, cells, speed, reach)
+    )(ratio, table, where, sums, *edges, inverse, cells, speed, reach)
 
 
 CORNERS = ((0, 0), (0, 1), (1, 0), (1, 1))
@@ -399,10 +403,14 @@
     return slice(row, row + META), slice(j % side * LANES, (j % side + 1) * LANES)
 
 
-def first_kernel(slabs, half, fl_ref, out_ref, table):
+def first_kernel(slabs, where, *refs):
+    piece_refs, (out_ref, fl_ref, table) = refs[:-3], refs[-3:]
     blocks, rows, share = fl_ref.shape
     lines = (rows - META_ROWS) // 2
-    flip = half[0]
+    mine = where[0] & (blocks - 1)
+    for m, piece in enumerate(piece_refs):
+        fl_ref[mine ^ m] = piece[...]
+    flip = where[0] // blocks
     flipped = flip == 1
     block = [k + flip * (blocks - 1 - 2 * k) for k in range(blocks)]
     entries, _ = half_chain(
@@ -437,26 +445,31 @@
         out_ref[rows, cols] = fl_ref[j, 2 * lines : 2 * lines + META, :LANES]
 
 
-def first_half(half, fl, slabs):
-    parts, rows, share = fl.shape
+def first_half(where, pieces, slabs):
+    parts = len(pieces)
+    rows, share = pieces[0].shape
     lines = (rows - META_ROWS) // 2
     vmem = pl.BlockSpec(memory_space=pltpu.VMEM)
-    rows = -(-meta_place(parts - 1, lines, share)[0].stop // ROWS) * ROWS
+    crossing = -(-meta_place(parts - 1, lines, share)[0].stop // ROWS) * ROWS
     return pl.pallas_call(
         functools.partial(first_kernel, slabs),
-        in_specs=[pl.BlockSpec(memory_space=pltpu.SMEM), vmem],
-        out_specs=vmem,
-        out_shape=jax.ShapeDtypeStruct((rows, share), jnp.float32),
+        in_specs=[pl.BlockSpec(memory_space=pltpu.SMEM)] + [vmem] * parts,
+        out_specs=[vmem, vmem],
+        out_shape=[
+            jax.ShapeDtypeStruct((crossing, share), jnp.float32),
+            jax.ShapeDtypeStruct((parts, rows, share), jnp.float32),
+        ],
         scratch_shapes=[pltpu.VMEM((parts, 2, ROWS, LANES), jnp.float32)],
         compiler_params=pltpu.CompilerParams(vmem_limit_bytes=SMALL_VMEM),
-        cost_estimate=pl.CostEstimate(flops=4 * fl.size, bytes_accessed=5 * fl.size, transcendentals=0),
+        cost_estimate=pl.CostEstimate(flops=10**6, bytes_accessed=10**6, transcendentals=0),
         name="reduced_in",
-    )(half, fl)
-
-
-def second_kernel(slabs, half, fl_ref, mine, other, uv_ref, info_ref, table):
+    )(where, *pieces)
+
+
+def second_kernel(slabs, where, fl_ref, mine, other, *refs):
+    out_refs, (info_ref, table, uv_ref) = refs[:-3], refs[-3:]
     blocks, _, lines, share = uv_ref.shape
-    flip = half[0]
+    flip = where[0] // blocks
     flipped = flip == 1
     block = [k + flip * (blocks - 1 - 2 * k) for k in range(blocks)]
     for j in range(blocks):
@@ -497,25 +510,28 @@
         return carry
 
     lax.fori_loop(0, lines // ROWS, group, 0)
-
-
-def second_half(half, fl, mine, other, slabs):
+    for m, out_ref in enumerate(out_refs):
+        out_ref[...] = uv_ref[(where[0] & (blocks - 1)) ^ m]
+
+
+def second_half(where, fl, mine, other, slabs):
     parts, rows, share = fl.shape
     lines = (rows - META_ROWS) // 2
     vmem = pl.BlockSpec(memory_space=pltpu.VMEM)
     return pl.pallas_call(
         functools.partial(second_kernel, slabs),
         in_specs=[pl.BlockSpec(memory_space=pltpu.SMEM), vmem, vmem, vmem],
-        out_specs=[vmem, vmem],
-        out_shape=[
-            jax.ShapeDtypeStruct((parts, 2, lines, share), jnp.float32),
-            jax.ShapeDtypeStruct((2 * parts, META_ROWS, LANES), jnp.float32),
+        out_specs=[vmem] * (parts + 1),
+        out_shape=[jax.ShapeDtypeStruct((2, lines, share), jnp.float32)] * parts
+        + [jax.ShapeDtypeStruct((2 * parts, META_ROWS, LANES), jnp.float32)],
+        scratch_shapes=[
+            pltpu.VMEM((parts + 1, len(KINDS), ROWS, LANES), jnp.float32),
+            pltpu.VMEM((parts, 2, lines, share), jnp.float32),
         ],
-        scratch_shapes=[pltpu.VMEM((parts + 1, len(KINDS), ROWS, LANES), jnp.float32)],
         compiler_params=pltpu.CompilerParams(vmem_limit_bytes=SMALL_VMEM),
         cost_estimate=pl.CostEstimate(flops=10 * fl.size, bytes_accessed=9 * fl.size, transcendentals=0),
         name="reduced_out",
-    )(half, fl, mine, other)
+    )(where, fl, mine, other)
 
 
 def extras_kernel(where_am_i, info, source, flux, inverse, inlet, holders, wells_ref, rows_ref, leaving, found):
@@ -562,7 +578,7 @@
         rows_ref[n] = dot(inverse[...], flux[n])
 
 
-def extras(depth_index, info, source, flux, inverse, inlet, holders):
+def extras(where, info, source, flux, inverse, inlet, holders):
     blocks = info.shape[0]
     _, slabs, span = flux.shape
     wells = source.shape[-1]
@@ -580,10 +596,13 @@
         compiler_params=pltpu.CompilerParams(vmem_limit_bytes=SMALL_VMEM),
         cost_estimate=pl.CostEstimate(flops=10**7, bytes_accessed=10**6, transcendentals=0),
         name="extras",
-    )(depth_index.reshape(1), info, source, flux, inverse, inlet, holders)
-
-
-def solve_kernel(right, uv, inverse, place_row, place_column, solved_wells, outer, out, factor, pick):
+    )(where, info, source, flux, inverse, inlet, holders)
+
+
+def solve_kernel(where, right, inverse, place_row, place_column, solved_wells, outer, *refs):
+    uv_refs, (out, factor, pick, uv) = refs[:-4], refs[-4:]
+    for m, piece in enumerate(uv_refs):
+        uv[(where[0] & (len(uv_refs) - 1)) ^ m] = piece[...]
     together, slabs, rows, span = right.shape
     wells = place_row.shape[1]
     step = pl.program_id(0)
@@ -652,38 +671,40 @@
                 out[z, line : line + 1, :] += outer[n, z : z + 1, :]
 
 
-def solve(right, uv, inverse, place_row, solved_wells, outer):
+def solve(where, right, uv, inverse, place_row, place_column, solved_wells, outer):
     groups, slabs, _, span = right.shape
     wells = place_row.shape[1]
     together = 2
     lines = together * ROWS
-    shares, _, _, share = uv.shape
+    _, _, share = uv[0].shape
     whole = lambda *shape: pl.BlockSpec(shape, lambda g: (0,) * len(shape))
     size = slabs * ROWS
     return pl.pallas_call(
         solve_kernel,
         grid=(groups // together,),
         in_specs=[
+            pl.BlockSpec(memory_space=pltpu.SMEM),
             pl.BlockSpec((together, slabs, ROWS, span), lambda g: (g, 0, 0, 0)),
-            pl.BlockSpec((shares, 2, lines, share), lambda g: (0, 0, g, 0)),
             whole(slabs, slabs),
             whole(1, wells),
             whole(wells, 1),
             whole(slabs, wells),
             whole(*outer.shape),
-        ],
+        ]
+        + [pl.BlockSpec((2, lines, share), lambda g: (0, g, 0))] * len(uv),
         out_specs=pl.BlockSpec((slabs, lines, span), lambda g: (0, g, 0)),
         out_shape=jax.ShapeDtypeStruct((slabs, groups * ROWS, span), jnp.float32),
         scratch_shapes=[
             pltpu.VMEM((size, 3 * size + 2 * wells), jnp.bfloat16),
             pltpu.VMEM((2 * wells, span), jnp.bfloat16),
+            pltpu.VMEM((len(uv), 2, lines, share), jnp.float32),
         ],
         compiler_params=pltpu.CompilerParams(vmem_limit_bytes=SOLVE_VMEM),
         cost_estimate=pl.CostEstimate(
             flops=8 * size * right.size, bytes_accessed=8 * right.size, transcendentals=0
         ),
         name="depth_solve",
-    )(right, uv, inverse, place_row, place_row.reshape(wells, 1), solved_wells, outer)
+    )(where, right, inverse, place_row, place_column, solved_wells, outer, *uv)
 
 
 def body(
@@ -706,12 +727,16 @@
     table = conductance_catalogue
 
     parts = depth_count // 2
-    halves = [list(range(h * parts, (h + 1) * parts)) for h in range(2)]
-    half = (depth_index // parts).astype(jnp.int32).reshape(1)
 
     place_row = well_position_inside.reshape(1, wells)
+    place_column = well_position_inside.reshape(wells, 1)
+    where = depth_index.reshape(1)
+    holders = lax.dynamic_slice_in_dim(well_holder_sequence, depth_index * owned, owned)
+    holders = holders.reshape(1, owned)
     first, last = edge_rows(warmth_before, stratum_category, table)
-    first, last, place_row = lax.optimization_barrier((first, last, place_row))
+    first, last, place_row, place_column, where, holders = lax.optimization_barrier(
+        (first, last, place_row, place_column, where, holders)
+    )
     count = lax.axis_size("strip")
     up = [(i, i + 1) for i in range(count - 1)]
     down = [(j, i) for i, j in up]
@@ -720,10 +745,10 @@
     right, sums, cells = stencil(
         warmth_before, stratum_category, table, pivot_matrix_reciprocal, place_row
     )
-    fl, flux, source = payload(
+    *pieces, flux, source = payload(
         linkage_factor,
         table,
-        depth_index,
+        where,
         sums,
         (first, last, before, after),
         pivot_matrix_reciprocal,
@@ -732,34 +757,30 @@
         well_reach.reshape(1, wells),
         parts,
     )
-    exchange = functools.partial(
-        lax.all_to_all,
-        axis_name="depth",
-        split_axis=0,
-        concat_axis=0,
-        tiled=True,
-        axis_index_groups=halves,
-    )
-    fl_all = exchange(fl)
-
-    mine = first_half(half, fl_all, slabs)
-    other = lax.ppermute(
-        mine, "depth", [(i, (i + parts) % depth_count) for i in range(depth_count)]
-    )
-    uv, info_all = second_half(half, fl_all, mine, other, slabs)
-    uv_own = exchange(uv)
-
-    holders = lax.dynamic_slice_in_dim(well_holder_sequence, depth_index * owned, owned)
+
+    def swapped(value, mask):
+        return lax.ppermute(value, "depth", [(i, i ^ mask) for i in range(depth_count)])
+
+    pieces = [swapped(pieces[m], m) for m in reversed(range(1, parts))][::-1] + [pieces[0]]
+    pieces = [pieces[-1]] + pieces[:-1]
+    mine, fl_all = first_half(where, pieces, slabs)
+    other = swapped(mine, parts)
+    *uv, info_all = second_half(where, fl_all, mine, other, slabs)
+    uv_own = [swapped(uv[m], m) for m in reversed(range(1, parts))][::-1]
+    uv_own = [uv[0]] + uv_own
+
     solved_wells, outer, leaving = extras(
-        depth_index,
+        where,
         info_all,
         source,
         flux,
         pivot_matrix_reciprocal,
         entering_warmth.reshape(1, wells),
-        holders.reshape(1, owned),
+        holders,
     )
-    solved = solve(right, uv_own, pivot_matrix_reciprocal, place_row, solved_wells, outer)
+    solved = solve(
+        where, right, uv_own, pivot_matrix_reciprocal, place_row, place_column, solved_wells, outer
+    )
     return solved, leaving.reshape(owned)
 
 

time: 80 us -> 77.5 us (0.969)
  local copies, waits for them, and re-layouts: 0.24 us -> 7.65 us
  Pallas kernels: 40.4 us -> 35.4 us
  waiting for transfers between devices: 21.9 us -> 17.2 us
    all_to_all x2 -> x0, waiting for transfers between devices: 17.2 us -> none  [the longest x1 10 us: body(): fl_all = exchange(fl)]
    ppermute x1 -> x7, waiting for transfers between devices: 4.75 us -> 17.2 us  [swapped(): lax.ppermute(value, 'depth', [(i, i ^ mask) for i in range(depth_count)])]
    all_to_all x2 -> x0, starting transfers between devices: 8.69 us -> none  [the longest x1 5.22 us: body(): fl_all = exchange(fl)]
    ppermute x1 -> x7, starting transfers between devices: 2.66 us -> 11.3 us  [swapped(): lax.ppermute(value, 'depth', [(i, i ^ mask) for i in range(depth_count)])]
    unnamed x18 -> x22, local copies, waits for them, and re-layouts: 0.05 us -> 7.46 us
    pallas_call x1, Pallas kernels: 9.78 us -> 7.12 us  [solve(): pl.pallas_call(solve_kernel, grid=(groups // together,), in_specs=[pl.Blo...]
    pallas_call x1, Pallas kernels: 23.1 us -> 22.3 us  [stencil(): pl.pallas_call(stencil_kernel, grid=(slabs // planes,), in_specs=[smem, s...]
  transfers between devices with their start and end apart: 5 -> 9, of which waited for: 3 -> 7; matrix products, arithmetic and copies ran while one was open for 0% -> 0% of each run, Pallas kernels for 30% -> 30%
where the time goes in v1:
time: 77.5 us; the launch traced here: 77.3 us
  Pallas kernels  35.4 us (46%)
  waiting for transfers between devices  17.2 us (22%)
  starting transfers between devices  15.6 us (20%)
  local copies, waits for them, and re-layouts  7.65 us (10%)
  between operations  1.45 us (2%)
    pallas_call x1, Pallas kernels, stencil(): pl.pallas_call(stencil_kernel, grid=(slabs // planes,), in_specs=[smem, s...  22.3 us
    ppermute x7, waiting for transfers between devices, swapped(): lax.ppermute(value, 'depth', [(i, i ^ mask) for i in range(depth_count)])  17.2 us
    ppermute x7, starting transfers between devices, swapped(): lax.ppermute(value, 'depth', [(i, i ^ mask) for i in range(depth_count)])  11.3 us
    unnamed x22, local copies, waits for them, and re-layouts  7.46 us
    pallas_call x1, Pallas kernels, solve(): pl.pallas_call(solve_kernel, grid=(groups // together,), in_specs=[pl.Blo...  7.12 us
    pallas_call x1, Pallas kernels, edge_rows(): pl.pallas_call(edge_kernel, grid=(1,), in_specs=[pl.BlockSpec(memory_spac...  3.35 us
    ppermute x1, starting transfers between devices, body(): before = lax.ppermute(last, 'strip', up)  3.05 us
  transfers between devices with their start and end apart: 9, of which 7 were waited for; matrix products, arithmetic and copies ran while one was open for 0% of the time, Pallas kernels for 30%

profile of v1, /device:TPU:0, one launch (start us, length us, event | category | flops | bytes accessed | tf_op | source)
XLA Modules:
  0.0 77.3 jit_solution(3768601344921024427)
XLA Ops:
  0.6 0.0 copy-start
  0.6 0.6 copy-done
  1.3 0.1 dynamic-slice_bitcast_fusion.holders
  1.4 0.0 copy-start.3
  1.4 0.0 copy-start.6
  1.4 0.0 copy-start.7
  1.4 3.4 %edge_rows.1 = (f32[2,32,1024]{2,1,0:T(8,128)}, f32[2,32,1024]{2,1,0:T(8,128)}) custom-call(f32[8]{0:T(128)} %table.5, f32[32,64,1024]{2,1,0:T(8,128)} %w_ref.1, s32[32,64,1024]{2,1,0:T(8,128)} %cat_ref.1, f32[32,64,1024]{2,1,0:T(8,128)} %w_ref.1, s32[32,64,1024]{2,1,0:T(8,128)} %cat_ref.1), custom_call_target="tpu_custom_call" | custom-call | flops 1000000 | bytes 2097152 | tf_op jit(solution)/shard_map/edge_rows/pallas_call | solution.py:67
  4.7 1.3 %collective-permute-start.1 = (f32[2,32,1024]{2,1,0:T(8,128)}, f32[2,32,1024]{2,1,0:T(8,128)S(1)}, u32[]{:S(2)}, u32[]{:S(2)}) collective-permute-start(f32[2,32,1024]{2,1,0:T(8,128)} %get-tuple-element.36.first), channel_id=1, source_target_pairs={{8,0},{16,8},{24,16},{9,1},{17,9},{25,17},{10,2},{18,10},{26,18},{... | collective-permute-start | bytes 786440 | tf_op jit(solution)/shard_map/ppermute | solution.py:744
  6.0 3.0 %collective-permute-start = (f32[2,32,1024]{2,1,0:T(8,128)}, f32[2,32,1024]{2,1,0:T(8,128)S(1)}, u32[]{:S(2)}, u32[]{:S(2)}) collective-permute-start(f32[2,32,1024]{2,1,0:T(8,128)} %get-tuple-element.37.last), channel_id=1, source_target_pairs={{0,8},{8,16},{16,24},{1,9},{9,17},{17,25},{2,10},{10,18},{18,26},{... | collective-permute-start | bytes 786440 | tf_op jit(solution)/shard_map/ppermute | solution.py:743
  9.7 0.0 copy-done.3
  9.7 0.0 copy-done.6
  9.7 0.0 copy-done.7
  9.7 0.0 copy-start.4
  9.8 0.0 copy-start.5
  9.8 0.0 copy-start.8
  9.8 0.0 copy-start.9
  9.8 0.0 copy-start.10
  9.8 22.3 %stencil.1 = (f32[8,32,8,1024]{3,2,1,0:T(8,128)S(1)}, f32[2,64,1024]{2,1,0:T(8,128)S(1)}, f32[2,32,128]{2,1,0:T(8,128)S(1)}) custom-call(f32[8]{0:T(128)S(1)} %copy-done.6, f32[32,32]{1,0:T(8,128)S(1)} %copy-done.3, f32[32,64,1024]{2,1,0:T(8,128)} %w_ref.1, s32[32,64,1024]{2,1,0:T(8,128)} %cat_ref.1, s32[1,128]{1,0:T(1,128)S(1)} %bitcast.9), custom_call_target="tpu_custom_call" | custom-call | flops 83886080 | bytes 25165824 | tf_op jit(solution)/shard_map/stencil/pallas_call | solution.py:194
  32.1 0.0 copy-start.1
  32.1 3.4 %copy-done.1 = f32[8,32,8,1024]{3,2,1,0:T(8,128)} copy-done((f32[8,32,8,1024]{3,2,1,0:T(8,128)}, f32[8,32,8,1024]{3,2,1,0:T(8,128)S(1)}, u32[]{:S(2)}) %copy-start.1) | copy-done | bytes 8388632
  35.5 0.0 collective-permute-done.1.after
  35.5 0.0 collective-permute-done.before
  35.5 0.0 copy-done.4
  35.5 0.0 copy-done.5
  35.5 0.0 copy-done.8
  35.5 0.0 copy-done.9
  35.5 1.0 %payload.1 = (f32[144,256]{1,0:T(8,128)S(1)}, f32[144,256]{1,0:T(8,128)S(1)}, f32[144,256]{1,0:T(8,128)S(1)}, f32[144,256]{1,0:T(8,128)S(1)}, f32[2,32,1024]{2,1,0:T(8,128)S(1)}, /*index=5*/f32[3,32,128]{2,1,0:T(8,128)S(1)}) custom-call(f32[1]{0:T(128)S(6)} %copy.13.ratio, f32[8]{0:T(128)S(1)} %copy-done.6, s32[1]{0:T(128)} %bitcast.2.where_am_i.where, ...), custom_call_target="tpu_custom_call" | custom-call | flops 1000000 | bytes 1000000 | tf_op jit(solution)/shard_map/payload/pallas_call | solution.py:303
  36.6 3.0 %collective-permute-start.2 = (f32[144,256]{1,0:T(8,128)S(1)}, f32[144,256]{1,0:T(8,128)S(1)}, u32[]{:S(2)}, u32[]{:S(2)}) collective-permute-start(f32[144,256]{1,0:T(8,128)S(1)} %get-tuple-element.40), channel_id=1, source_target_pairs={{0,1},{1,0},{2,3},{3,2},{4,5},{5,4},{6,7},{7,6},{8,9},{9,8},{10,11... | collective-permute-start | bytes 442376 | tf_op jit(solution)/shard_map/ppermute | solution.py:762
  39.6 1.6 %collective-permute-start.3 = (f32[144,256]{1,0:T(8,128)S(1)}, f32[144,256]{1,0:T(8,128)S(1)}, u32[]{:S(2)}, u32[]{:S(2)}) collective-permute-start(f32[144,256]{1,0:T(8,128)S(1)} %get-tuple-element.41), channel_id=1, source_target_pairs={{0,2},{1,3},{2,0},{3,1},{4,6},{5,7},{6,4},{7,5},{8,10},{9,11},{10,... | collective-permute-start | bytes 442376 | tf_op jit(solution)/shard_map/ppermute | solution.py:762
  41.1 0.0 collective-permute-start.4
  41.1 2.5 %collective-permute-done.2.refs_1_ = f32[144,256]{1,0:T(8,128)S(1)} collective-permute-done((f32[144,256]{1,0:T(8,128)S(1)}, f32[144,256]{1,0:T(8,128)S(1)}, u32[]{:S(2)}, u32[]{:S(2)}) %collective-permute-start.2) | collective-permute-done | bytes 147488 | tf_op jit(solution)/shard_map/ppermute | solution.py:762
  43.6 2.6 %collective-permute-done.3.refs_2_ = f32[144,256]{1,0:T(8,128)S(1)} collective-permute-done((f32[144,256]{1,0:T(8,128)S(1)}, f32[144,256]{1,0:T(8,128)S(1)}, u32[]{:S(2)}, u32[]{:S(2)}) %collective-permute-start.3) | collective-permute-done | bytes 147488 | tf_op jit(solution)/shard_map/ppermute | solution.py:762
  46.3 2.5 %collective-permute-done.4.refs_3_ = f32[144,256]{1,0:T(8,128)S(1)} collective-permute-done((f32[144,256]{1,0:T(8,128)S(1)}, f32[144,256]{1,0:T(8,128)S(1)}, u32[]{:S(2)}, u32[]{:S(2)}) %collective-permute-start.4) | collective-permute-done | bytes 147488 | tf_op jit(solution)/shard_map/ppermute | solution.py:762
  48.8 0.3 reduced_in.1
  49.2 3.1 %collective-permute-start.5 = (f32[88,256]{1,0:T(8,128)S(1)}, f32[88,256]{1,0:T(8,128)S(1)}, u32[]{:S(2)}, u32[]{:S(2)}) collective-permute-start(f32[88,256]{1,0:T(8,128)S(1)} %get-tuple-element.44.mine), channel_id=1, source_target_pairs={{0,4},{1,5},{2,6},{3,7},{4,0},{5,1},{6,2},{7,3},{8,12},{9,13},{10,... | collective-permute-start | bytes 270344 | tf_op jit(solution)/shard_map/ppermute | solution.py:762
  52.3 4.7 %collective-permute-done.5.other = f32[88,256]{1,0:T(8,128)S(1)} collective-permute-done((f32[88,256]{1,0:T(8,128)S(1)}, f32[88,256]{1,0:T(8,128)S(1)}, u32[]{:S(2)}, u32[]{:S(2)}) %collective-permute-start.5) | collective-permute-done | bytes 90144 | tf_op jit(solution)/shard_map/ppermute | solution.py:762
  57.0 0.5 reduced_out.1
  57.5 1.6 %collective-permute-start.6 = (f32[2,64,256]{2,1,0:T(8,128)S(1)}, f32[2,64,256]{2,1,0:T(8,128)S(1)}, u32[]{:S(2)}, u32[]{:S(2)}) collective-permute-start(f32[2,64,256]{2,1,0:T(8,128)S(1)} %get-tuple-element.52), channel_id=1, source_target_pairs={{0,1},{1,0},{2,3},{3,2},{4,5},{5,4},{6,7},{7,6},{8,9},{9,8},{10,11... | collective-permute-start | bytes 393224 | tf_op jit(solution)/shard_map/ppermute | solution.py:762
  59.1 0.7 collective-permute-start.7
  59.8 1.3 %collective-permute-start.8 = (f32[2,64,256]{2,1,0:T(8,128)S(1)}, f32[2,64,256]{2,1,0:T(8,128)S(1)}, u32[]{:S(2)}, u32[]{:S(2)}) collective-permute-start(f32[2,64,256]{2,1,0:T(8,128)S(1)} %get-tuple-element.54), channel_id=1, source_target_pairs={{0,3},{1,2},{2,1},{3,0},{4,7},{5,6},{6,5},{7,4},{8,11},{9,10},{10,... | collective-permute-start | bytes 393224 | tf_op jit(solution)/shard_map/ppermute | solution.py:762
  61.1 0.1 copy.12.place_column
  61.2 0.0 copy-done.10
  61.2 0.8 %extras.1 = (f32[32,128]{1,0:T(8,128)S(1)}, f32[2,32,1024]{2,1,0:T(8,128)S(1)}, f32[1,16]{1,0:T(1,128)}) custom-call(s32[1]{0:T(128)} %bitcast.2.where_am_i.where, f32[8,16,128]{2,1,0:T(8,128)S(1)} %get-tuple-element.45.info, f32[3,32,128]{2,1,0:T(8,128)S(1)} %get-tuple-element.46.source, f32[2,32,1024]{2,1,0:T(8,128)S(1)} %get-tuple-element.47.flux, ...), custom_call_target="tpu_custom_call" | custom-call | flops 10000000 | bytes 1000000 | tf_op jit(solution)/shard_map/extras/pallas_call | solution.py:586
  62.0 1.1 %collective-permute-done.6.refs_1_ = f32[2,64,256]{2,1,0:T(8,128)S(1)} collective-permute-done((f32[2,64,256]{2,1,0:T(8,128)S(1)}, f32[2,64,256]{2,1,0:T(8,128)S(1)}, u32[]{:S(2)}, u32[]{:S(2)}) %collective-permute-start.6) | collective-permute-done | bytes 131104 | tf_op jit(solution)/shard_map/ppermute | solution.py:762
  63.1 1.6 %collective-permute-done.7.refs_2_ = f32[2,64,256]{2,1,0:T(8,128)S(1)} collective-permute-done((f32[2,64,256]{2,1,0:T(8,128)S(1)}, f32[2,64,256]{2,1,0:T(8,128)S(1)}, u32[]{:S(2)}, u32[]{:S(2)}) %collective-permute-start.7) | collective-permute-done | bytes 131104 | tf_op jit(solution)/shard_map/ppermute | solution.py:762
  64.6 2.2 %collective-permute-done.8.refs_3_ = f32[2,64,256]{2,1,0:T(8,128)S(1)} collective-permute-done((f32[2,64,256]{2,1,0:T(8,128)S(1)}, f32[2,64,256]{2,1,0:T(8,128)S(1)}, u32[]{:S(2)}, u32[]{:S(2)}) %collective-permute-start.8) | collective-permute-done | bytes 131104 | tf_op jit(solution)/shard_map/ppermute | solution.py:762
  66.8 3.4 %copy-done.2 = f32[8,32,8,1024]{3,2,1,0:T(8,128)S(1)} copy-done((f32[8,32,8,1024]{3,2,1,0:T(8,128)S(1)}, f32[8,32,8,1024]{3,2,1,0:T(8,128)}, u32[]{:S(2)}) %copy-start.2) | copy-done | bytes 8388632
  70.2 7.1 %depth_solve.1 = f32[32,64,1024]{2,1,0:T(8,128)} custom-call(s32[1]{0:T(128)} %bitcast.2.where_am_i.where, f32[8,32,8,1024]{3,2,1,0:T(8,128)S(1)} %copy-done.2, f32[32,32]{1,0:T(8,128)S(1)} %copy-done.3, s32[1,128]{1,0:T(1,128)S(1)} %bitcast.11, s32[128,1]{1,0:T(8,128)S(1)} %copy.12.place_column, f32[32,128]{1,0:T(8,128)S(1)} %get-tuple-element.49.solved_wells, ...), custom_call_target="tpu_custom_call" | custom-call | flops 4294967296 | bytes 16777216 | tf_op jit(solution)/shard_map/depth_solve/pallas_call | solution.py:682
  (1 shorter events, 0.0 us)
Async XLA Ops:
  0.6 0.7 copy-start
  1.4 8.3 %copy-start.3 = (f32[32,32]{1,0:T(8,128)S(1)}, f32[32,32]{1,0:T(8,128)}, u32[]{:S(2)}) copy-start(f32[32,32]{1,0:T(8,128)} %inverse.5) | copy-start | bytes 12292
  1.4 8.4 %copy-start.6 = (f32[8]{0:T(128)S(1)}, f32[8]{0:T(128)}, u32[]{:S(2)}) copy-start(f32[8]{0:T(128)} %table.5) | copy-start | bytes 100
  1.4 8.4 %copy-start.7 = (s32[128]{0:T(128)S(1)}, s32[128]{0:T(128)}, u32[]{:S(2)}) copy-start(s32[128]{0:T(128)} %param.15) | copy-start | bytes 1540
  4.7 30.7 %collective-permute-start.1 = (f32[2,32,1024]{2,1,0:T(8,128)}, f32[2,32,1024]{2,1,0:T(8,128)S(1)}, u32[]{:S(2)}, u32[]{:S(2)}) collective-permute-start(f32[2,32,1024]{2,1,0:T(8,128)} %get-tuple-element.36.first), channel_id=1, source_target_pairs={{8,0},{16,8},{24,16},{9,1},{17,9},{25,17},{10,2},{18,10},{26,18},{... | collective-permute-start | bytes 786440 | tf_op jit(solution)/shard_map/ppermute | solution.py:744
  6.0 29.5 %collective-permute-start = (f32[2,32,1024]{2,1,0:T(8,128)}, f32[2,32,1024]{2,1,0:T(8,128)S(1)}, u32[]{:S(2)}, u32[]{:S(2)}) collective-permute-start(f32[2,32,1024]{2,1,0:T(8,128)} %get-tuple-element.37.last), channel_id=1, source_target_pairs={{0,8},{8,16},{16,24},{1,9},{9,17},{17,25},{2,10},{10,18},{18,26},{... | collective-permute-start | bytes 786440 | tf_op jit(solution)/shard_map/ppermute | solution.py:743
  9.7 25.7 %copy-start.4 = (f32[2,32,1024]{2,1,0:T(8,128)S(1)}, f32[2,32,1024]{2,1,0:T(8,128)}, u32[]{:S(2)}) copy-start(f32[2,32,1024]{2,1,0:T(8,128)} %get-tuple-element.36.first) | copy-start | bytes 786436
  9.8 25.7 %copy-start.5 = (f32[2,32,1024]{2,1,0:T(8,128)S(1)}, f32[2,32,1024]{2,1,0:T(8,128)}, u32[]{:S(2)}) copy-start(f32[2,32,1024]{2,1,0:T(8,128)} %get-tuple-element.37.last) | copy-start | bytes 786436
  9.8 25.7 %copy-start.8 = (f32[128]{0:T(128)S(1)}, f32[128]{0:T(128)}, u32[]{:S(2)}) copy-start(f32[128]{0:T(128)} %param.19) | copy-start | bytes 1540
  9.8 25.7 %copy-start.9 = (s32[128]{0:T(128)S(1)}, s32[128]{0:T(128)}, u32[]{:S(2)}) copy-start(s32[128]{0:T(128)} %param.17) | copy-start | bytes 1540
  9.8 51.4 %copy-start.10 = (f32[128]{0:T(128)S(1)}, f32[128]{0:T(128)}, u32[]{:S(2)}) copy-start(f32[128]{0:T(128)} %param.18) | copy-start | bytes 1540
  32.1 3.4 %copy-start.1 = (f32[8,32,8,1024]{3,2,1,0:T(8,128)}, f32[8,32,8,1024]{3,2,1,0:T(8,128)S(1)}, u32[]{:S(2)}) copy-start(f32[8,32,8,1024]{3,2,1,0:T(8,128)S(1)} %get-tuple-element.33.right) | copy-start | bytes 25165828
  36.6 7.1 %collective-permute-start.2 = (f32[144,256]{1,0:T(8,128)S(1)}, f32[144,256]{1,0:T(8,128)S(1)}, u32[]{:S(2)}, u32[]{:S(2)}) collective-permute-start(f32[144,256]{1,0:T(8,128)S(1)} %get-tuple-element.40), channel_id=1, source_target_pairs={{0,1},{1,0},{2,3},{3,2},{4,5},{5,4},{6,7},{7,6},{8,9},{9,8},{10,11... | collective-permute-start | bytes 442376 | tf_op jit(solution)/shard_map/ppermute | solution.py:762
  39.6 6.7 %collective-permute-start.3 = (f32[144,256]{1,0:T(8,128)S(1)}, f32[144,256]{1,0:T(8,128)S(1)}, u32[]{:S(2)}, u32[]{:S(2)}) collective-permute-start(f32[144,256]{1,0:T(8,128)S(1)} %get-tuple-element.41), channel_id=1, source_target_pairs={{0,2},{1,3},{2,0},{3,1},{4,6},{5,7},{6,4},{7,5},{8,10},{9,11},{10,... | collective-permute-start | bytes 442376 | tf_op jit(solution)/shard_map/ppermute | solution.py:762
  41.1 7.7 %collective-permute-start.4 = (f32[144,256]{1,0:T(8,128)S(1)}, f32[144,256]{1,0:T(8,128)S(1)}, u32[]{:S(2)}, u32[]{:S(2)}) collective-permute-start(f32[144,256]{1,0:T(8,128)S(1)} %get-tuple-element.42), channel_id=1, source_target_pairs={{0,3},{1,2},{2,1},{3,0},{4,7},{5,6},{6,5},{7,4},{8,11},{9,10},{10,... | collective-permute-start | bytes 442376 | tf_op jit(solution)/shard_map/ppermute | solution.py:762
  49.2 7.8 %collective-permute-start.5 = (f32[88,256]{1,0:T(8,128)S(1)}, f32[88,256]{1,0:T(8,128)S(1)}, u32[]{:S(2)}, u32[]{:S(2)}) collective-permute-start(f32[88,256]{1,0:T(8,128)S(1)} %get-tuple-element.44.mine), channel_id=1, source_target_pairs={{0,4},{1,5},{2,6},{3,7},{4,0},{5,1},{6,2},{7,3},{8,12},{9,13},{10,... | collective-permute-start | bytes 270344 | tf_op jit(solution)/shard_map/ppermute | solution.py:762
  57.5 5.5 %collective-permute-start.6 = (f32[2,64,256]{2,1,0:T(8,128)S(1)}, f32[2,64,256]{2,1,0:T(8,128)S(1)}, u32[]{:S(2)}, u32[]{:S(2)}) collective-permute-start(f32[2,64,256]{2,1,0:T(8,128)S(1)} %get-tuple-element.52), channel_id=1, source_target_pairs={{0,1},{1,0},{2,3},{3,2},{4,5},{5,4},{6,7},{7,6},{8,9},{9,8},{10,11... | collective-permute-start | bytes 393224 | tf_op jit(solution)/shard_map/ppermute | solution.py:762
  59.1 5.5 %collective-permute-start.7 = (f32[2,64,256]{2,1,0:T(8,128)S(1)}, f32[2,64,256]{2,1,0:T(8,128)S(1)}, u32[]{:S(2)}, u32[]{:S(2)}) collective-permute-start(f32[2,64,256]{2,1,0:T(8,128)S(1)} %get-tuple-element.53), channel_id=1, source_target_pairs={{0,2},{1,3},{2,0},{3,1},{4,6},{5,7},{6,4},{7,5},{8,10},{9,11},{10,... | collective-permute-start | bytes 393224 | tf_op jit(solution)/shard_map/ppermute | solution.py:762
  59.8 7.0 %collective-permute-start.8 = (f32[2,64,256]{2,1,0:T(8,128)S(1)}, f32[2,64,256]{2,1,0:T(8,128)S(1)}, u32[]{:S(2)}, u32[]{:S(2)}) collective-permute-start(f32[2,64,256]{2,1,0:T(8,128)S(1)} %get-tuple-element.54), channel_id=1, source_target_pairs={{0,3},{1,2},{2,1},{3,0},{4,7},{5,6},{6,5},{7,4},{8,11},{9,10},{10,... | collective-permute-start | bytes 393224 | tf_op jit(solution)/shard_map/ppermute | solution.py:762
  66.8 3.4 %copy-start.2 = (f32[8,32,8,1024]{3,2,1,0:T(8,128)S(1)}, f32[8,32,8,1024]{3,2,1,0:T(8,128)}, u32[]{:S(2)}) copy-start(f32[8,32,8,1024]{3,2,1,0:T(8,128)} %copy-done.1) | copy-start | bytes 25165828

commit v2 on v1

--- a/solution.py
+++ b/solution.py
@@ -548,8 +548,12 @@
     for j in reversed(range(blocks)):
         rise[j] = value
         value = row_of(j, 0) * value + row_of(j, 2)
-    held = holders[...] == lax.broadcasted_iota(jnp.int32, (wells, holders.shape[1]), 0)
-    leaving[...] = dot(jnp.broadcast_to(value, (ROWS, wells)), held.astype(jnp.float32))[0:1]
+    held = holders[...] == lax.broadcasted_iota(jnp.int32, (wells, wells), 0)
+    ordered = dot(jnp.broadcast_to(value, (ROWS, wells)), held.astype(jnp.float32))
+    owned = leaving.shape[1]
+    source_lane = lax.broadcasted_iota(jnp.int32, (wells, owned), 0)
+    mine = source_lane == d * owned + lax.broadcasted_iota(jnp.int32, (wells, owned), 1)
+    leaving[...] = dot(ordered, mine.astype(jnp.float32))[0:1]
 
     ends = [
         [row_of(j, n) + row_of(j, n + 1) * down[j] + row_of(j, n + 2) * rise[j] for j in range(blocks)]
@@ -590,7 +594,7 @@
         out_shape=[
             jax.ShapeDtypeStruct((slabs, wells), jnp.float32),
             jax.ShapeDtypeStruct((2, slabs, span), jnp.float32),
-            jax.ShapeDtypeStruct((1, holders.shape[1]), jnp.float32),
+            jax.ShapeDtypeStruct((1, wells // blocks), jnp.float32),
         ],
         scratch_shapes=[pltpu.VMEM((blocks, ROWS, wells), jnp.float32)],
         compiler_params=pltpu.CompilerParams(vmem_limit_bytes=SMALL_VMEM),
@@ -599,7 +603,7 @@
     )(where, info, source, flux, inverse, inlet, holders)
 
 
-def solve_kernel(where, right, inverse, place_row, place_column, solved_wells, outer, *refs):
+def solve_kernel(where, right, inverse, place_row, solved_wells, outer, *refs):
     uv_refs, (out, factor, pick, uv) = refs[:-4], refs[-4:]
     for m, piece in enumerate(uv_refs):
         uv[(where[0] & (len(uv_refs) - 1)) ^ m] = piece[...]
@@ -631,8 +635,12 @@
                 factor[:, size : 2 * size] = wide
             else:
                 factor[:, 2 * size : 3 * size] = wide
-        column = lax.broadcasted_iota(jnp.int32, (wells, span), 1)
-        chosen = (column == place_column[...] % span).astype(jnp.float32).astype(jnp.bfloat16)
+        across = lax.broadcasted_iota(jnp.int32, (wells, wells), 1)
+        diagonal = lax.broadcasted_iota(jnp.int32, (wells, wells), 0) == across
+        place = jnp.where(diagonal, (place_row[...] % span).astype(jnp.float32), 0.0)
+        place = jnp.sum(place, axis=1, keepdims=True)
+        column = lax.broadcasted_iota(jnp.int32, (wells, span), 1).astype(jnp.float32)
+        chosen = (column == place).astype(jnp.float32).astype(jnp.bfloat16)
         pick[:wells] = chosen
         pick[wells:] = chosen
 
@@ -671,7 +679,7 @@
                 out[z, line : line + 1, :] += outer[n, z : z + 1, :]
 
 
-def solve(where, right, uv, inverse, place_row, place_column, solved_wells, outer):
+def solve(where, right, uv, inverse, place_row, solved_wells, outer):
     groups, slabs, _, span = right.shape
     wells = place_row.shape[1]
     together = 2
@@ -687,7 +695,6 @@
             pl.BlockSpec((together, slabs, ROWS, span), lambda g: (g, 0, 0, 0)),
             whole(slabs, slabs),
             whole(1, wells),
-            whole(wells, 1),
             whole(slabs, wells),
             whole(*outer.shape),
         ]
@@ -704,7 +711,7 @@
             flops=8 * size * right.size, bytes_accessed=8 * right.size, transcendentals=0
         ),
         name="depth_solve",
-    )(where, right, inverse, place_row, place_column, solved_wells, outer, *uv)
+    )(where, right, inverse, place_row, solved_wells, outer, *uv)
 
 
 def body(
@@ -729,14 +736,9 @@
     parts = depth_count // 2
 
     place_row = well_position_inside.reshape(1, wells)
-    place_column = well_position_inside.reshape(wells, 1)
     where = depth_index.reshape(1)
-    holders = lax.dynamic_slice_in_dim(well_holder_sequence, depth_index * owned, owned)
-    holders = holders.reshape(1, owned)
     first, last = edge_rows(warmth_before, stratum_category, table)
-    first, last, place_row, place_column, where, holders = lax.optimization_barrier(
-        (first, last, place_row, place_column, where, holders)
-    )
+    first, last, place_row, where = lax.optimization_barrier((first, last, place_row, where))
     count = lax.axis_size("strip")
     up = [(i, i + 1) for i in range(count - 1)]
     down = [(j, i) for i, j in up]
@@ -776,11 +778,9 @@
         flux,
         pivot_matrix_reciprocal,
         entering_warmth.reshape(1, wells),
-        holders,
+        well_holder_sequence.reshape(1, wells),
     )
-    solved = solve(
-        where, right, uv_own, pivot_matrix_reciprocal, place_row, place_column, solved_wells, outer
-    )
+    solved = solve(where, right, uv_own, pivot_matrix_reciprocal, place_row, solved_wells, outer)
     return solved, leaving.reshape(owned)
 
 

time: 77.5 us -> 70.1 us (0.905)
  local copies, waits for them, and re-layouts: 7.65 us -> 0.05 us
    unnamed x22 -> x18, local copies, waits for them, and re-layouts: 7.46 us -> 0.05 us
  transfers between devices with their start and end apart: 9 -> 9, of which waited for: 7 -> 7; matrix products, arithmetic and copies ran while one was open for 0% -> 0% of each run, Pallas kernels for 30% -> 33%
where the time goes in v2:
time: 70.1 us; the launch traced here: 69.9 us
  Pallas kernels  35.6 us (51%)
  waiting for transfers between devices  17.2 us (25%)
  starting transfers between devices  15.6 us (22%)
  between operations  1.48 us (2%)
    pallas_call x1, Pallas kernels, stencil(): pl.pallas_call(stencil_kernel, grid=(slabs // planes,), in_specs=[smem, s...  22.3 us
    ppermute x7, waiting for transfers between devices, swapped(): lax.ppermute(value, 'depth', [(i, i ^ mask) for i in range(depth_count)])  17.2 us
    ppermute x7, starting transfers between devices, swapped(): lax.ppermute(value, 'depth', [(i, i ^ mask) for i in range(depth_count)])  11.3 us
    pallas_call x1, Pallas kernels, solve(): pl.pallas_call(solve_kernel, grid=(groups // together,), in_specs=[pl.Blo...  7.16 us
    pallas_call x1, Pallas kernels, edge_rows(): pl.pallas_call(edge_kernel, grid=(1,), in_specs=[pl.BlockSpec(memory_spac...  3.32 us
    ppermute x1, starting transfers between devices, body(): before = lax.ppermute(last, 'strip', up)  3.05 us
  transfers between devices with their start and end apart: 9, of which 7 were waited for; matrix products, arithmetic and copies ran while one was open for 0% of the time, Pallas kernels for 33%

profile of v2, /device:TPU:0, one launch (start us, length us, event | category | flops | bytes accessed | tf_op | source)
XLA Modules:
  0.0 69.9 jit_solution(8937385530965857601)
XLA Ops:
  0.6 0.0 copy-start.2
  0.6 0.0 copy-start.3
  0.7 0.0 copy-start.4
  0.7 3.3 %edge_rows.1 = (f32[2,32,1024]{2,1,0:T(8,128)}, f32[2,32,1024]{2,1,0:T(8,128)}) custom-call(f32[8]{0:T(128)} %table.5, f32[32,64,1024]{2,1,0:T(8,128)} %w_ref.1, s32[32,64,1024]{2,1,0:T(8,128)} %cat_ref.1, f32[32,64,1024]{2,1,0:T(8,128)} %w_ref.1, s32[32,64,1024]{2,1,0:T(8,128)} %cat_ref.1), custom_call_target="tpu_custom_call" | custom-call | flops 1000000 | bytes 2097152 | tf_op jit(solution)/shard_map/edge_rows/pallas_call | solution.py:67
  4.0 1.3 %collective-permute-start.1 = (f32[2,32,1024]{2,1,0:T(8,128)}, f32[2,32,1024]{2,1,0:T(8,128)S(1)}, u32[]{:S(2)}, u32[]{:S(2)}) collective-permute-start(f32[2,32,1024]{2,1,0:T(8,128)} %get-tuple-element.33.first), channel_id=1, source_target_pairs={{8,0},{16,8},{24,16},{9,1},{17,9},{25,17},{10,2},{18,10},{26,18},{... | collective-permute-start | bytes 786440 | tf_op jit(solution)/shard_map/ppermute | solution.py:746
  5.3 3.0 %collective-permute-start = (f32[2,32,1024]{2,1,0:T(8,128)}, f32[2,32,1024]{2,1,0:T(8,128)S(1)}, u32[]{:S(2)}, u32[]{:S(2)}) collective-permute-start(f32[2,32,1024]{2,1,0:T(8,128)} %get-tuple-element.34.last), channel_id=1, source_target_pairs={{0,8},{8,16},{16,24},{1,9},{9,17},{17,25},{2,10},{10,18},{18,26},{... | collective-permute-start | bytes 786440 | tf_op jit(solution)/shard_map/ppermute | solution.py:745
  9.0 0.0 copy-done.2
  9.0 0.0 copy-done.3
  9.0 0.0 copy-done.4
  9.0 0.0 copy-start
  9.0 0.0 copy-start.1
  9.0 0.0 copy-start.5
  9.0 0.0 copy-start.6
  9.1 0.0 copy-start.7
  9.1 0.0 copy-start.8
  9.1 22.3 %stencil.1 = (f32[8,32,8,1024]{3,2,1,0:T(8,128)S(1)}, f32[2,64,1024]{2,1,0:T(8,128)S(1)}, f32[2,32,128]{2,1,0:T(8,128)S(1)}) custom-call(f32[8]{0:T(128)S(1)} %copy-done.3, f32[32,32]{1,0:T(8,128)S(1)} %copy-done.2, f32[32,64,1024]{2,1,0:T(8,128)} %w_ref.1, s32[32,64,1024]{2,1,0:T(8,128)} %cat_ref.1, s32[1,128]{1,0:T(1,128)S(1)} %bitcast.7), custom_call_target="tpu_custom_call" | custom-call | flops 83886080 | bytes 25165824 | tf_op jit(solution)/shard_map/stencil/pallas_call | solution.py:194
  31.3 0.0 collective-permute-done.1.after
  31.4 0.0 collective-permute-done.before
  31.4 0.0 copy-done
  31.4 0.0 copy-done.1
  31.4 0.0 copy-done.5
  31.4 0.0 copy-done.6
  31.4 1.0 %payload.1 = (f32[144,256]{1,0:T(8,128)S(1)}, f32[144,256]{1,0:T(8,128)S(1)}, f32[144,256]{1,0:T(8,128)S(1)}, f32[144,256]{1,0:T(8,128)S(1)}, f32[2,32,1024]{2,1,0:T(8,128)S(1)}, /*index=5*/f32[3,32,128]{2,1,0:T(8,128)S(1)}) custom-call(f32[1]{0:T(128)S(6)} %copy.12.ratio, f32[8]{0:T(128)S(1)} %copy-done.3, s32[1]{0:T(128)} %bitcast.1.where_am_i.where, ...), custom_call_target="tpu_custom_call" | custom-call | flops 1000000 | bytes 1000000 | tf_op jit(solution)/shard_map/payload/pallas_call | solution.py:303
  32.5 3.0 %collective-permute-start.2 = (f32[144,256]{1,0:T(8,128)S(1)}, f32[144,256]{1,0:T(8,128)S(1)}, u32[]{:S(2)}, u32[]{:S(2)}) collective-permute-start(f32[144,256]{1,0:T(8,128)S(1)} %get-tuple-element.37), channel_id=1, source_target_pairs={{0,1},{1,0},{2,3},{3,2},{4,5},{5,4},{6,7},{7,6},{8,9},{9,8},{10,11... | collective-permute-start | bytes 442376 | tf_op jit(solution)/shard_map/ppermute | solution.py:764
  35.5 1.6 %collective-permute-start.3 = (f32[144,256]{1,0:T(8,128)S(1)}, f32[144,256]{1,0:T(8,128)S(1)}, u32[]{:S(2)}, u32[]{:S(2)}) collective-permute-start(f32[144,256]{1,0:T(8,128)S(1)} %get-tuple-element.38), channel_id=1, source_target_pairs={{0,2},{1,3},{2,0},{3,1},{4,6},{5,7},{6,4},{7,5},{8,10},{9,11},{10,... | collective-permute-start | bytes 442376 | tf_op jit(solution)/shard_map/ppermute | solution.py:764
  37.0 0.0 collective-permute-start.4
  37.0 2.5 %collective-permute-done.2.refs_1_ = f32[144,256]{1,0:T(8,128)S(1)} collective-permute-done((f32[144,256]{1,0:T(8,128)S(1)}, f32[144,256]{1,0:T(8,128)S(1)}, u32[]{:S(2)}, u32[]{:S(2)}) %collective-permute-start.2) | collective-permute-done | bytes 147488 | tf_op jit(solution)/shard_map/ppermute | solution.py:764
  39.5 2.6 %collective-permute-done.3.refs_2_ = f32[144,256]{1,0:T(8,128)S(1)} collective-permute-done((f32[144,256]{1,0:T(8,128)S(1)}, f32[144,256]{1,0:T(8,128)S(1)}, u32[]{:S(2)}, u32[]{:S(2)}) %collective-permute-start.3) | collective-permute-done | bytes 147488 | tf_op jit(solution)/shard_map/ppermute | solution.py:764
  42.2 2.5 %collective-permute-done.4.refs_3_ = f32[144,256]{1,0:T(8,128)S(1)} collective-permute-done((f32[144,256]{1,0:T(8,128)S(1)}, f32[144,256]{1,0:T(8,128)S(1)}, u32[]{:S(2)}, u32[]{:S(2)}) %collective-permute-start.4) | collective-permute-done | bytes 147488 | tf_op jit(solution)/shard_map/ppermute | solution.py:764
  44.7 0.3 reduced_in.1
  45.1 3.1 %collective-permute-start.5 = (f32[88,256]{1,0:T(8,128)S(1)}, f32[88,256]{1,0:T(8,128)S(1)}, u32[]{:S(2)}, u32[]{:S(2)}) collective-permute-start(f32[88,256]{1,0:T(8,128)S(1)} %get-tuple-element.41.mine), channel_id=1, source_target_pairs={{0,4},{1,5},{2,6},{3,7},{4,0},{5,1},{6,2},{7,3},{8,12},{9,13},{10,... | collective-permute-start | bytes 270344 | tf_op jit(solution)/shard_map/ppermute | solution.py:764
  48.2 4.7 %collective-permute-done.5.other = f32[88,256]{1,0:T(8,128)S(1)} collective-permute-done((f32[88,256]{1,0:T(8,128)S(1)}, f32[88,256]{1,0:T(8,128)S(1)}, u32[]{:S(2)}, u32[]{:S(2)}) %collective-permute-start.5) | collective-permute-done | bytes 90144 | tf_op jit(solution)/shard_map/ppermute | solution.py:764
  52.9 0.5 reduced_out.1
  53.4 1.6 %collective-permute-start.6 = (f32[2,64,256]{2,1,0:T(8,128)S(1)}, f32[2,64,256]{2,1,0:T(8,128)S(1)}, u32[]{:S(2)}, u32[]{:S(2)}) collective-permute-start(f32[2,64,256]{2,1,0:T(8,128)S(1)} %get-tuple-element.48), channel_id=1, source_target_pairs={{0,1},{1,0},{2,3},{3,2},{4,5},{5,4},{6,7},{7,6},{8,9},{9,8},{10,11... | collective-permute-start | bytes 393224 | tf_op jit(solution)/shard_map/ppermute | solution.py:764
  55.0 0.7 collective-permute-start.7
  55.7 1.3 %collective-permute-start.8 = (f32[2,64,256]{2,1,0:T(8,128)S(1)}, f32[2,64,256]{2,1,0:T(8,128)S(1)}, u32[]{:S(2)}, u32[]{:S(2)}) collective-permute-start(f32[2,64,256]{2,1,0:T(8,128)S(1)} %get-tuple-element.50), channel_id=1, source_target_pairs={{0,3},{1,2},{2,1},{3,0},{4,7},{5,6},{6,5},{7,4},{8,11},{9,10},{10,... | collective-permute-start | bytes 393224 | tf_op jit(solution)/shard_map/ppermute | solution.py:764
  57.0 0.0 copy-done.7
  57.0 0.0 copy-done.8
  57.0 1.0 %extras.1 = (f32[32,128]{1,0:T(8,128)S(1)}, f32[2,32,1024]{2,1,0:T(8,128)S(1)}, f32[1,16]{1,0:T(1,128)}) custom-call(s32[1]{0:T(128)} %bitcast.1.where_am_i.where, f32[8,16,128]{2,1,0:T(8,128)S(1)} %get-tuple-element.42.info, f32[3,32,128]{2,1,0:T(8,128)S(1)} %get-tuple-element.43.source, f32[2,32,1024]{2,1,0:T(8,128)S(1)} %get-tuple-element.44.flux, ...), custom_call_target="tpu_custom_call" | custom-call | flops 10000000 | bytes 1000000 | tf_op jit(solution)/shard_map/extras/pallas_call | solution.py:590
  57.9 1.0 %collective-permute-done.6.refs_1_ = f32[2,64,256]{2,1,0:T(8,128)S(1)} collective-permute-done((f32[2,64,256]{2,1,0:T(8,128)S(1)}, f32[2,64,256]{2,1,0:T(8,128)S(1)}, u32[]{:S(2)}, u32[]{:S(2)}) %collective-permute-start.6) | collective-permute-done | bytes 131104 | tf_op jit(solution)/shard_map/ppermute | solution.py:764
  59.0 1.6 %collective-permute-done.7.refs_2_ = f32[2,64,256]{2,1,0:T(8,128)S(1)} collective-permute-done((f32[2,64,256]{2,1,0:T(8,128)S(1)}, f32[2,64,256]{2,1,0:T(8,128)S(1)}, u32[]{:S(2)}, u32[]{:S(2)}) %collective-permute-start.7) | collective-permute-done | bytes 131104 | tf_op jit(solution)/shard_map/ppermute | solution.py:764
  60.5 2.2 %collective-permute-done.8.refs_3_ = f32[2,64,256]{2,1,0:T(8,128)S(1)} collective-permute-done((f32[2,64,256]{2,1,0:T(8,128)S(1)}, f32[2,64,256]{2,1,0:T(8,128)S(1)}, u32[]{:S(2)}, u32[]{:S(2)}) %collective-permute-start.8) | collective-permute-done | bytes 131104 | tf_op jit(solution)/shard_map/ppermute | solution.py:764
  62.7 7.2 %depth_solve.1 = f32[32,64,1024]{2,1,0:T(8,128)} custom-call(s32[1]{0:T(128)} %bitcast.1.where_am_i.where, f32[8,32,8,1024]{3,2,1,0:T(8,128)S(1)} %get-tuple-element.31.right, f32[32,32]{1,0:T(8,128)S(1)} %copy-done.2, s32[1,128]{1,0:T(1,128)S(1)} %bitcast.8, f32[32,128]{1,0:T(8,128)S(1)} %get-tuple-element.45.solved_wells, ...), custom_call_target="tpu_custom_call" | custom-call | flops 4294967296 | bytes 16777216 | tf_op jit(solution)/shard_map/depth_solve/pallas_call | solution.py:690
Async XLA Ops:
  0.6 8.3 %copy-start.2 = (f32[32,32]{1,0:T(8,128)S(1)}, f32[32,32]{1,0:T(8,128)}, u32[]{:S(2)}) copy-start(f32[32,32]{1,0:T(8,128)} %inverse.5) | copy-start | bytes 12292
  0.6 8.3 %copy-start.3 = (f32[8]{0:T(128)S(1)}, f32[8]{0:T(128)}, u32[]{:S(2)}) copy-start(f32[8]{0:T(128)} %table.5) | copy-start | bytes 100
  0.7 8.3 %copy-start.4 = (s32[128]{0:T(128)S(1)}, s32[128]{0:T(128)}, u32[]{:S(2)}) copy-start(s32[128]{0:T(128)} %param.15) | copy-start | bytes 1540
  4.0 27.4 %collective-permute-start.1 = (f32[2,32,1024]{2,1,0:T(8,128)}, f32[2,32,1024]{2,1,0:T(8,128)S(1)}, u32[]{:S(2)}, u32[]{:S(2)}) collective-permute-start(f32[2,32,1024]{2,1,0:T(8,128)} %get-tuple-element.33.first), channel_id=1, source_target_pairs={{8,0},{16,8},{24,16},{9,1},{17,9},{25,17},{10,2},{18,10},{26,18},{... | collective-permute-start | bytes 786440 | tf_op jit(solution)/shard_map/ppermute | solution.py:746
  5.3 26.1 %collective-permute-start = (f32[2,32,1024]{2,1,0:T(8,128)}, f32[2,32,1024]{2,1,0:T(8,128)S(1)}, u32[]{:S(2)}, u32[]{:S(2)}) collective-permute-start(f32[2,32,1024]{2,1,0:T(8,128)} %get-tuple-element.34.last), channel_id=1, source_target_pairs={{0,8},{8,16},{16,24},{1,9},{9,17},{17,25},{2,10},{10,18},{18,26},{... | collective-permute-start | bytes 786440 | tf_op jit(solution)/shard_map/ppermute | solution.py:745
  9.0 22.4 %copy-start = (f32[2,32,1024]{2,1,0:T(8,128)S(1)}, f32[2,32,1024]{2,1,0:T(8,128)}, u32[]{:S(2)}) copy-start(f32[2,32,1024]{2,1,0:T(8,128)} %get-tuple-element.33.first) | copy-start | bytes 786436
  9.0 22.4 %copy-start.1 = (f32[2,32,1024]{2,1,0:T(8,128)S(1)}, f32[2,32,1024]{2,1,0:T(8,128)}, u32[]{:S(2)}) copy-start(f32[2,32,1024]{2,1,0:T(8,128)} %get-tuple-element.34.last) | copy-start | bytes 786436
  9.0 22.4 %copy-start.5 = (f32[128]{0:T(128)S(1)}, f32[128]{0:T(128)}, u32[]{:S(2)}) copy-start(f32[128]{0:T(128)} %param.19) | copy-start | bytes 1540
  9.0 22.4 %copy-start.6 = (s32[128]{0:T(128)S(1)}, s32[128]{0:T(128)}, u32[]{:S(2)}) copy-start(s32[128]{0:T(128)} %param.17) | copy-start | bytes 1540
  9.1 47.9 %copy-start.7 = (f32[128]{0:T(128)S(1)}, f32[128]{0:T(128)}, u32[]{:S(2)}) copy-start(f32[128]{0:T(128)} %param.18) | copy-start | bytes 1540
  9.1 47.9 %copy-start.8 = (s32[128]{0:T(128)S(1)}, s32[128]{0:T(128)}, u32[]{:S(2)}) copy-start(s32[128]{0:T(128)} %param.16) | copy-start | bytes 1540
  32.5 7.1 %collective-permute-start.2 = (f32[144,256]{1,0:T(8,128)S(1)}, f32[144,256]{1,0:T(8,128)S(1)}, u32[]{:S(2)}, u32[]{:S(2)}) collective-permute-start(f32[144,256]{1,0:T(8,128)S(1)} %get-tuple-element.37), channel_id=1, source_target_pairs={{0,1},{1,0},{2,3},{3,2},{4,5},{5,4},{6,7},{7,6},{8,9},{9,8},{10,11... | collective-permute-start | bytes 442376 | tf_op jit(solution)/shard_map/ppermute | solution.py:764
  35.5 6.7 %collective-permute-start.3 = (f32[144,256]{1,0:T(8,128)S(1)}, f32[144,256]{1,0:T(8,128)S(1)}, u32[]{:S(2)}, u32[]{:S(2)}) collective-permute-start(f32[144,256]{1,0:T(8,128)S(1)} %get-tuple-element.38), channel_id=1, source_target_pairs={{0,2},{1,3},{2,0},{3,1},{4,6},{5,7},{6,4},{7,5},{8,10},{9,11},{10,... | collective-permute-start | bytes 442376 | tf_op jit(solution)/shard_map/ppermute | solution.py:764
  37.0 7.7 %collective-permute-start.4 = (f32[144,256]{1,0:T(8,128)S(1)}, f32[144,256]{1,0:T(8,128)S(1)}, u32[]{:S(2)}, u32[]{:S(2)}) collective-permute-start(f32[144,256]{1,0:T(8,128)S(1)} %get-tuple-element.39), channel_id=1, source_target_pairs={{0,3},{1,2},{2,1},{3,0},{4,7},{5,6},{6,5},{7,4},{8,11},{9,10},{10,... | collective-permute-start | bytes 442376 | tf_op jit(solution)/shard_map/ppermute | solution.py:764
  45.1 7.8 %collective-permute-start.5 = (f32[88,256]{1,0:T(8,128)S(1)}, f32[88,256]{1,0:T(8,128)S(1)}, u32[]{:S(2)}, u32[]{:S(2)}) collective-permute-start(f32[88,256]{1,0:T(8,128)S(1)} %get-tuple-element.41.mine), channel_id=1, source_target_pairs={{0,4},{1,5},{2,6},{3,7},{4,0},{5,1},{6,2},{7,3},{8,12},{9,13},{10,... | collective-permute-start | bytes 270344 | tf_op jit(solution)/shard_map/ppermute | solution.py:764
  53.4 5.5 %collective-permute-start.6 = (f32[2,64,256]{2,1,0:T(8,128)S(1)}, f32[2,64,256]{2,1,0:T(8,128)S(1)}, u32[]{:S(2)}, u32[]{:S(2)}) collective-permute-start(f32[2,64,256]{2,1,0:T(8,128)S(1)} %get-tuple-element.48), channel_id=1, source_target_pairs={{0,1},{1,0},{2,3},{3,2},{4,5},{5,4},{6,7},{7,6},{8,9},{9,8},{10,11... | collective-permute-start | bytes 393224 | tf_op jit(solution)/shard_map/ppermute | solution.py:764
  55.0 5.5 %collective-permute-start.7 = (f32[2,64,256]{2,1,0:T(8,128)S(1)}, f32[2,64,256]{2,1,0:T(8,128)S(1)}, u32[]{:S(2)}, u32[]{:S(2)}) collective-permute-start(f32[2,64,256]{2,1,0:T(8,128)S(1)} %get-tuple-element.49), channel_id=1, source_target_pairs={{0,2},{1,3},{2,0},{3,1},{4,6},{5,7},{6,4},{7,5},{8,10},{9,11},{10,... | collective-permute-start | bytes 393224 | tf_op jit(solution)/shard_map/ppermute | solution.py:764
  55.7 7.0 %collective-permute-start.8 = (f32[2,64,256]{2,1,0:T(8,128)S(1)}, f32[2,64,256]{2,1,0:T(8,128)S(1)}, u32[]{:S(2)}, u32[]{:S(2)}) collective-permute-start(f32[2,64,256]{2,1,0:T(8,128)S(1)} %get-tuple-element.50), channel_id=1, source_target_pairs={{0,3},{1,2},{2,1},{3,0},{4,7},{5,6},{6,5},{7,4},{8,11},{9,10},{10,... | collective-permute-start | bytes 393224 | tf_op jit(solution)/shard_map/ppermute | solution.py:764

commit v3 on v2

--- a/solution.py
+++ b/solution.py
@@ -30,6 +30,15 @@
         ]
         bit *= 2
     return values[0]
+
+
+def crossed(mask):
+    return mask & ~3 | (mask & 1) << 1 | (mask & 2) >> 1
+
+
+def partner(where, mask, blocks):
+    odd = where[1] & 1 if blocks >= 4 else 0
+    return (where[0] & (blocks - 1)) ^ (mask + odd * (crossed(mask) - mask))
 
 
 def split_bf16(value, pieces):
@@ -243,7 +252,6 @@
     out_refs, (flux_ref, source_ref, keep, force, paths, totals) = refs[:-6], refs[-6:]
     copies = len(out_refs)
     share = out_refs[0].shape[1]
-    mine = where_am_i[0] & (copies - 1)
     _, lines, span = sums.shape
     _, slabs, wells = cells.shape
     dot = functools.partial(jnp.dot, precision=HIGHEST, preferred_element_type=jnp.float32)
@@ -283,7 +291,7 @@
         for q in range(2):
             totals[q, line : line + 1, :] += extra[q : q + 1]
     for m, out_ref in enumerate(out_refs):
-        cols = pl.ds(pl.multiple_of((mine ^ m) * share, share), share)
+        cols = pl.ds(pl.multiple_of(partner(where_am_i, m, copies) * share, share), share)
         for q in range(2):
             out_ref[q * lines : (q + 1) * lines] = totals[q, :, cols]
         out_ref[meta : meta + META_ROWS] = jnp.zeros((META_ROWS, share), jnp.float32)
@@ -407,9 +415,8 @@
     piece_refs, (out_ref, fl_ref, table) = refs[:-3], refs[-3:]
     blocks, rows, share = fl_ref.shape
     lines = (rows - META_ROWS) // 2
-    mine = where[0] & (blocks - 1)
     for m, piece in enumerate(piece_refs):
-        fl_ref[mine ^ m] = piece[...]
+        fl_ref[partner(where, m, blocks)] = piece[...]
     flip = where[0] // blocks
     flipped = flip == 1
     block = [k + flip * (blocks - 1 - 2 * k) for k in range(blocks)]
@@ -511,7 +518,7 @@
 
     lax.fori_loop(0, lines // ROWS, group, 0)
     for m, out_ref in enumerate(out_refs):
-        out_ref[...] = uv_ref[(where[0] & (blocks - 1)) ^ m]
+        out_ref[...] = uv_ref[partner(where, m, blocks)]
 
 
 def second_half(where, fl, mine, other, slabs):
@@ -606,8 +613,9 @@
 def solve_kernel(where, right, inverse, place_row, solved_wells, outer, *refs):
     uv_refs, (out, factor, pick, uv) = refs[:-4], refs[-4:]
     for m, piece in enumerate(uv_refs):
-        uv[(where[0] & (len(uv_refs) - 1)) ^ m] = piece[...]
-    together, slabs, rows, span = right.shape
+        uv[partner(where, m, len(uv_refs))] = piece[...]
+    _, slabs, rows, span = right.shape
+    together = out.shape[1] // rows
     wells = place_row.shape[1]
     step = pl.program_id(0)
     size = slabs * rows
@@ -646,7 +654,8 @@
 
     tile = min(span, 256)
     for n in range(together):
-        line = lax.broadcasted_iota(jnp.int32, (slabs, rows, wells), 1) + (step * together + n) * rows
+        group = step * together + n
+        line = lax.broadcasted_iota(jnp.int32, (slabs, rows, wells), 1) + group * rows
         at_wells = jnp.where(line == (place_row[...] // span)[None], solved_wells[...][:, None, :], 0.0)
         at_wells = jnp.concatenate(split_bf16(at_wells.reshape(size, wells), 2), axis=1)
         factor[:, 3 * size :] = at_wells
@@ -657,9 +666,9 @@
             cols = slice(t * tile, (t + 1) * tile)
             value = jnp.concatenate(
                 [
-                    right[n, 0:1, :, cols] + above[None, :, cols],
-                    right[n, 1 : slabs - 1, :, cols],
-                    right[n, slabs - 1 :, :, cols] + below[None, :, cols],
+                    right[group, 0:1, :, cols] + above[None, :, cols],
+                    right[group, 1 : slabs - 1, :, cols],
+                    right[group, slabs - 1 :, :, cols] + below[None, :, cols],
                 ],
                 axis=0,
             ).reshape(size, tile)
@@ -692,7 +701,7 @@
         grid=(groups // together,),
         in_specs=[
             pl.BlockSpec(memory_space=pltpu.SMEM),
-            pl.BlockSpec((together, slabs, ROWS, span), lambda g: (g, 0, 0, 0)),
+            pl.BlockSpec(memory_space=pltpu.VMEM),
             whole(slabs, slabs),
             whole(1, wells),
             whole(slabs, wells),
@@ -736,7 +745,7 @@
     parts = depth_count // 2
 
     place_row = well_position_inside.reshape(1, wells)
-    where = depth_index.reshape(1)
+    where = jnp.stack([depth_index, lax.axis_index("strip")])
     first, last = edge_rows(warmth_before, stratum_category, table)
     first, last, place_row, where = lax.optimization_barrier((first, last, place_row, where))
     count = lax.axis_size("strip")
@@ -763,12 +772,20 @@
     def swapped(value, mask):
         return lax.ppermute(value, "depth", [(i, i ^ mask) for i in range(depth_count)])
 
-    pieces = [swapped(pieces[m], m) for m in reversed(range(1, parts))][::-1] + [pieces[0]]
+    def with_partner(value, mask):
+        perm = []
+        for strip in range(count):
+            step = crossed(mask) if strip % 2 and parts >= 4 else mask
+            start = strip * depth_count
+            perm += [(start + i, start + (i ^ step)) for i in range(depth_count)]
+        return lax.ppermute(value, ("strip", "depth"), perm)
+
+    pieces = [with_partner(pieces[m], m) for m in reversed(range(1, parts))][::-1] + [pieces[0]]
     pieces = [pieces[-1]] + pieces[:-1]
     mine, fl_all = first_half(where, pieces, slabs)
     other = swapped(mine, parts)
     *uv, info_all = second_half(where, fl_all, mine, other, slabs)
-    uv_own = [swapped(uv[m], m) for m in reversed(range(1, parts))][::-1]
+    uv_own = [with_partner(uv[m], m) for m in reversed(range(1, parts))][::-1]
     uv_own = [uv[0]] + uv_own
 
     solved_wells, outer, leaving = extras(

time: 70.1 us -> 70.7 us (level)
  Pallas kernels: 35.6 us -> 37.8 us
  waiting for transfers between devices: 17.2 us -> 16 us
    ppermute x7 -> x1, waiting for transfers between devices: 17.2 us -> 4.76 us  [swapped(): lax.ppermute(value, 'depth', [(i, i ^ mask) for i in range(depth_count)])]
    ppermute x0 -> x6, waiting for transfers between devices: none -> 11.2 us  [with_partner(): return lax.ppermute(value, ('strip', 'depth'), perm)]
    ppermute x7 -> x1, starting transfers between devices: 11.3 us -> 2.78 us  [swapped(): lax.ppermute(value, 'depth', [(i, i ^ mask) for i in range(depth_count)])]
    ppermute x0 -> x6, starting transfers between devices: none -> 8.13 us  [with_partner(): return lax.ppermute(value, ('strip', 'depth'), perm)]
  transfers between devices with their start and end apart: 9 -> 9, of which waited for: 7 -> 5; matrix products, arithmetic and copies ran while one was open for 0% -> 0% of each run, Pallas kernels for 33% -> 34%
where the time goes in v3:
time: 70.7 us; the launch traced here: 70.5 us
  Pallas kernels  37.8 us (53%)
  waiting for transfers between devices  16 us (23%)
  starting transfers between devices  15.2 us (21%)
  between operations  1.47 us (2%)
    pallas_call x1, Pallas kernels, stencil(): pl.pallas_call(stencil_kernel, grid=(slabs // planes,), in_specs=[smem, s...  22.3 us
    ppermute x6, waiting for transfers between devices, with_partner(): return lax.ppermute(value, ('strip', 'depth'), perm)  11.2 us
    ppermute x6, starting transfers between devices, with_partner(): return lax.ppermute(value, ('strip', 'depth'), perm)  8.13 us
    pallas_call x1, Pallas kernels, solve(): pl.pallas_call(solve_kernel, grid=(groups // together,), in_specs=[pl.Blo...  7.68 us
    ppermute x1, waiting for transfers between devices, swapped(): lax.ppermute(value, 'depth', [(i, i ^ mask) for i in range(depth_count)])  4.76 us
    pallas_call x1, Pallas kernels, edge_rows(): pl.pallas_call(edge_kernel, grid=(1,), in_specs=[pl.BlockSpec(memory_spac...  3.34 us
    ppermute x1, starting transfers between devices, body(): before = lax.ppermute(last, 'strip', up)  3.05 us
    ppermute x1, starting transfers between devices, swapped(): lax.ppermute(value, 'depth', [(i, i ^ mask) for i in range(depth_count)])  2.78 us
  transfers between devices with their start and end apart: 9, of which 5 were waited for; matrix products, arithmetic and copies ran while one was open for 0% of the time, Pallas kernels for 34%

profile of v3, /device:TPU:0, one launch (start us, length us, event | category | flops | bytes accessed | tf_op | source)
XLA Modules:
  0.0 70.5 jit_solution(1749177755468893294)
XLA Ops:
  0.6 0.1 pad_add_fusion.where_am_i.where
  0.7 0.0 copy-start.2
  0.7 0.0 copy-start.3
  0.7 0.0 copy-start.4
  0.7 3.3 %edge_rows.1 = (f32[2,32,1024]{2,1,0:T(8,128)}, f32[2,32,1024]{2,1,0:T(8,128)}) custom-call(f32[8]{0:T(128)} %table.5, f32[32,64,1024]{2,1,0:T(8,128)} %w_ref.1, s32[32,64,1024]{2,1,0:T(8,128)} %cat_ref.1, f32[32,64,1024]{2,1,0:T(8,128)} %w_ref.1, s32[32,64,1024]{2,1,0:T(8,128)} %cat_ref.1), custom_call_target="tpu_custom_call" | custom-call | flops 1000000 | bytes 2097152 | tf_op jit(solution)/shard_map/edge_rows/pallas_call | solution.py:76
  4.1 1.3 %collective-permute-start.1 = (f32[2,32,1024]{2,1,0:T(8,128)}, f32[2,32,1024]{2,1,0:T(8,128)S(1)}, u32[]{:S(2)}, u32[]{:S(2)}) collective-permute-start(f32[2,32,1024]{2,1,0:T(8,128)} %get-tuple-element.33.first), channel_id=1, source_target_pairs={{8,0},{16,8},{24,16},{9,1},{17,9},{25,17},{10,2},{18,10},{26,18},{... | collective-permute-start | bytes 786440 | tf_op jit(solution)/shard_map/ppermute | solution.py:755
  5.3 3.0 %collective-permute-start = (f32[2,32,1024]{2,1,0:T(8,128)}, f32[2,32,1024]{2,1,0:T(8,128)S(1)}, u32[]{:S(2)}, u32[]{:S(2)}) collective-permute-start(f32[2,32,1024]{2,1,0:T(8,128)} %get-tuple-element.34.last), channel_id=1, source_target_pairs={{0,8},{8,16},{16,24},{1,9},{9,17},{17,25},{2,10},{10,18},{18,26},{... | collective-permute-start | bytes 786440 | tf_op jit(solution)/shard_map/ppermute | solution.py:754
  9.0 0.0 copy-done.2
  9.1 0.0 copy-done.3
  9.1 0.0 copy-done.4
  9.1 0.0 copy-start
  9.1 0.0 copy-start.1
  9.1 0.0 copy-start.5
  9.1 0.0 copy-start.6
  9.1 0.0 copy-start.7
  9.1 0.0 copy-start.8
  9.1 22.3 %stencil.1 = (f32[8,32,8,1024]{3,2,1,0:T(8,128)S(1)}, f32[2,64,1024]{2,1,0:T(8,128)S(1)}, f32[2,32,128]{2,1,0:T(8,128)S(1)}) custom-call(f32[8]{0:T(128)S(1)} %copy-done.3, f32[32,32]{1,0:T(8,128)S(1)} %copy-done.2, f32[32,64,1024]{2,1,0:T(8,128)} %w_ref.1, s32[32,64,1024]{2,1,0:T(8,128)} %cat_ref.1, s32[1,128]{1,0:T(1,128)S(1)} %bitcast.8), custom_call_target="tpu_custom_call" | custom-call | flops 83886080 | bytes 25165824 | tf_op jit(solution)/shard_map/stencil/pallas_call | solution.py:203
  31.4 0.0 collective-permute-done.1.after
  31.4 0.0 collective-permute-done.before
  31.4 0.0 copy-done
  31.4 0.0 copy-done.1
  31.5 0.0 copy-done.5
  31.5 0.0 copy-done.6
  31.5 1.0 %payload.1 = (f32[144,256]{1,0:T(8,128)S(1)}, f32[144,256]{1,0:T(8,128)S(1)}, f32[144,256]{1,0:T(8,128)S(1)}, f32[144,256]{1,0:T(8,128)S(1)}, f32[2,32,1024]{2,1,0:T(8,128)S(1)}, /*index=5*/f32[3,32,128]{2,1,0:T(8,128)S(1)}) custom-call(f32[1]{0:T(128)S(6)} %copy.12.ratio, f32[8]{0:T(128)S(1)} %copy-done.3, s32[2]{0:T(128)S(1)} %pad_add_fusion.where_am_i.where, ...), custom_call_target="tpu_custom_call" | custom-call | flops 1000000 | bytes 1000000 | tf_op jit(solution)/shard_map/payload/pallas_call | solution.py:311
  32.5 3.0 %collective-permute-start.2 = (f32[144,256]{1,0:T(8,128)S(1)}, f32[144,256]{1,0:T(8,128)S(1)}, u32[]{:S(2)}, u32[]{:S(2)}) collective-permute-start(f32[144,256]{1,0:T(8,128)S(1)} %get-tuple-element.37), channel_id=1, source_target_pairs={{0,1},{1,0},{2,3},{3,2},{4,5},{5,4},{6,7},{7,6},{8,10},{9,11},{10,... | collective-permute-start | bytes 442376 | tf_op jit(solution)/shard_map/ppermute | solution.py:781
  35.5 1.6 %collective-permute-start.3 = (f32[144,256]{1,0:T(8,128)S(1)}, f32[144,256]{1,0:T(8,128)S(1)}, u32[]{:S(2)}, u32[]{:S(2)}) collective-permute-start(f32[144,256]{1,0:T(8,128)S(1)} %get-tuple-element.38), channel_id=1, source_target_pairs={{0,2},{1,3},{2,0},{3,1},{4,6},{5,7},{6,4},{7,5},{8,9},{9,8},{10,11... | collective-permute-start | bytes 442376 | tf_op jit(solution)/shard_map/ppermute | solution.py:781
  37.1 0.0 collective-permute-start.4
  37.1 1.5 %collective-permute-done.2.refs_1_ = f32[144,256]{1,0:T(8,128)S(1)} collective-permute-done((f32[144,256]{1,0:T(8,128)S(1)}, f32[144,256]{1,0:T(8,128)S(1)}, u32[]{:S(2)}, u32[]{:S(2)}) %collective-permute-start.2) | collective-permute-done | bytes 147488 | tf_op jit(solution)/shard_map/ppermute | solution.py:781
  38.7 2.9 %collective-permute-done.3.refs_2_ = f32[144,256]{1,0:T(8,128)S(1)} collective-permute-done((f32[144,256]{1,0:T(8,128)S(1)}, f32[144,256]{1,0:T(8,128)S(1)}, u32[]{:S(2)}, u32[]{:S(2)}) %collective-permute-start.3) | collective-permute-done | bytes 147488 | tf_op jit(solution)/shard_map/ppermute | solution.py:781
  41.6 3.3 %collective-permute-done.4.refs_3_ = f32[144,256]{1,0:T(8,128)S(1)} collective-permute-done((f32[144,256]{1,0:T(8,128)S(1)}, f32[144,256]{1,0:T(8,128)S(1)}, u32[]{:S(2)}, u32[]{:S(2)}) %collective-permute-start.4) | collective-permute-done | bytes 147488 | tf_op jit(solution)/shard_map/ppermute | solution.py:781
  44.9 0.9 %reduced_in.1 = (f32[88,256]{1,0:T(8,128)S(1)}, f32[4,144,256]{2,1,0:T(8,128)S(1)}) custom-call(s32[2]{0:T(128)S(1)} %pad_add_fusion.where_am_i.where, f32[144,256]{1,0:T(8,128)S(1)} %get-tuple-element.36.refs_0_, f32[144,256]{1,0:T(8,128)S(1)} %collective-permute-done.2.refs_1_, f32[144,256]{1,0:T(8,128)S(1)} %collective-permute-done.3.refs_2_, ...), custom_call_target="tpu_custom_call" | custom-call | flops 1000000 | bytes 1000000 | tf_op jit(solution)/shard_map/reduced_in/pallas_call | solution.py:461
  45.8 2.8 %collective-permute-start.5 = (f32[88,256]{1,0:T(8,128)S(1)}, f32[88,256]{1,0:T(8,128)S(1)}, u32[]{:S(2)}, u32[]{:S(2)}) collective-permute-start(f32[88,256]{1,0:T(8,128)S(1)} %get-tuple-element.41.mine), channel_id=1, source_target_pairs={{0,4},{1,5},{2,6},{3,7},{4,0},{5,1},{6,2},{7,3},{8,12},{9,13},{10,... | collective-permute-start | bytes 270344 | tf_op jit(solution)/shard_map/ppermute | solution.py:773
  48.6 4.8 %collective-permute-done.5.other = f32[88,256]{1,0:T(8,128)S(1)} collective-permute-done((f32[88,256]{1,0:T(8,128)S(1)}, f32[88,256]{1,0:T(8,128)S(1)}, u32[]{:S(2)}, u32[]{:S(2)}) %collective-permute-start.5) | collective-permute-done | bytes 90144 | tf_op jit(solution)/shard_map/ppermute | solution.py:773
  53.3 1.1 %reduced_out.1 = (f32[2,64,256]{2,1,0:T(8,128)S(1)}, f32[2,64,256]{2,1,0:T(8,128)S(1)}, f32[2,64,256]{2,1,0:T(8,128)S(1)}, f32[2,64,256]{2,1,0:T(8,128)S(1)}, f32[8,16,128]{2,1,0:T(8,128)S(1)}) custom-call(s32[2]{0:T(128)S(1)} %pad_add_fusion.where_am_i.where, f32[4,144,256]{2,1,0:T(8,128)S(1)} %get-tuple-element.40.fl_ref, ...), custom_call_target="tpu_custom_call" | custom-call | flops 1474560 | bytes 1327104 | tf_op jit(solution)/shard_map/reduced_out/pallas_call | solution.py:528
  54.4 0.1 collective-permute-start.6
  54.5 0.6 collective-permute-start.7
  55.1 2.9 %collective-permute-start.8 = (f32[2,64,256]{2,1,0:T(8,128)S(1)}, f32[2,64,256]{2,1,0:T(8,128)S(1)}, u32[]{:S(2)}, u32[]{:S(2)}) collective-permute-start(f32[2,64,256]{2,1,0:T(8,128)S(1)} %get-tuple-element.50), channel_id=1, source_target_pairs={{0,3},{1,2},{2,1},{3,0},{4,7},{5,6},{6,5},{7,4},{8,11},{9,10},{10,... | collective-permute-start | bytes 393224 | tf_op jit(solution)/shard_map/ppermute | solution.py:781
  57.9 0.0 copy-done.7
  58.0 0.0 copy-done.8
  58.0 1.5 %extras.1 = (f32[32,128]{1,0:T(8,128)S(1)}, f32[2,32,1024]{2,1,0:T(8,128)S(1)}, f32[1,16]{1,0:T(1,128)}) custom-call(s32[2]{0:T(128)S(1)} %pad_add_fusion.where_am_i.where, f32[8,16,128]{2,1,0:T(8,128)S(1)} %get-tuple-element.42.info, f32[3,32,128]{2,1,0:T(8,128)S(1)} %get-tuple-element.43.source, f32[2,32,1024]{2,1,0:T(8,128)S(1)} %get-tuple-element.44.flux, ...), custom_call_target="tpu_custom_call" | custom-call | flops 10000000 | bytes 1000000 | tf_op jit(solution)/shard_map/extras/pallas_call | solution.py:597
  59.5 3.4 %collective-permute-done.6.refs_1_ = f32[2,64,256]{2,1,0:T(8,128)S(1)} collective-permute-done((f32[2,64,256]{2,1,0:T(8,128)S(1)}, f32[2,64,256]{2,1,0:T(8,128)S(1)}, u32[]{:S(2)}, u32[]{:S(2)}) %collective-permute-start.6) | collective-permute-done | bytes 131104 | tf_op jit(solution)/shard_map/ppermute | solution.py:781
  62.9 0.0 collective-permute-done.7.refs_2_
  62.9 0.0 collective-permute-done.8.refs_3_
  62.9 7.7 %depth_solve.1 = f32[32,64,1024]{2,1,0:T(8,128)} custom-call(s32[2]{0:T(128)S(1)} %pad_add_fusion.where_am_i.where, f32[8,32,8,1024]{3,2,1,0:T(8,128)S(1)} %get-tuple-element.31.right, f32[32,32]{1,0:T(8,128)S(1)} %copy-done.2, s32[1,128]{1,0:T(1,128)S(1)} %bitcast.9, f32[32,128]{1,0:T(8,128)S(1)} %get-tuple-element.45.solved_wells, ...), custom_call_target="tpu_custom_call" | custom-call | flops 4294967296 | bytes 16777216 | tf_op jit(solution)/shard_map/depth_solve/pallas_call | solution.py:699
Async XLA Ops:
  0.7 8.3 %copy-start.2 = (f32[32,32]{1,0:T(8,128)S(1)}, f32[32,32]{1,0:T(8,128)}, u32[]{:S(2)}) copy-start(f32[32,32]{1,0:T(8,128)} %inverse.5) | copy-start | bytes 12292
  0.7 8.3 %copy-start.3 = (f32[8]{0:T(128)S(1)}, f32[8]{0:T(128)}, u32[]{:S(2)}) copy-start(f32[8]{0:T(128)} %table.5) | copy-start | bytes 100
  0.7 8.4 %copy-start.4 = (s32[128]{0:T(128)S(1)}, s32[128]{0:T(128)}, u32[]{:S(2)}) copy-start(s32[128]{0:T(128)} %param.15) | copy-start | bytes 1540
  4.1 27.4 %collective-permute-start.1 = (f32[2,32,1024]{2,1,0:T(8,128)}, f32[2,32,1024]{2,1,0:T(8,128)S(1)}, u32[]{:S(2)}, u32[]{:S(2)}) collective-permute-start(f32[2,32,1024]{2,1,0:T(8,128)} %get-tuple-element.33.first), channel_id=1, source_target_pairs={{8,0},{16,8},{24,16},{9,1},{17,9},{25,17},{10,2},{18,10},{26,18},{... | collective-permute-start | bytes 786440 | tf_op jit(solution)/shard_map/ppermute | solution.py:755
  5.3 26.1 %collective-permute-start = (f32[2,32,1024]{2,1,0:T(8,128)}, f32[2,32,1024]{2,1,0:T(8,128)S(1)}, u32[]{:S(2)}, u32[]{:S(2)}) collective-permute-start(f32[2,32,1024]{2,1,0:T(8,128)} %get-tuple-element.34.last), channel_id=1, source_target_pairs={{0,8},{8,16},{16,24},{1,9},{9,17},{17,25},{2,10},{10,18},{18,26},{... | collective-permute-start | bytes 786440 | tf_op jit(solution)/shard_map/ppermute | solution.py:754
  9.1 22.4 %copy-start = (f32[2,32,1024]{2,1,0:T(8,128)S(1)}, f32[2,32,1024]{2,1,0:T(8,128)}, u32[]{:S(2)}) copy-start(f32[2,32,1024]{2,1,0:T(8,128)} %get-tuple-element.33.first) | copy-start | bytes 786436
  9.1 22.4 %copy-start.1 = (f32[2,32,1024]{2,1,0:T(8,128)S(1)}, f32[2,32,1024]{2,1,0:T(8,128)}, u32[]{:S(2)}) copy-start(f32[2,32,1024]{2,1,0:T(8,128)} %get-tuple-element.34.last) | copy-start | bytes 786436
  9.1 22.4 %copy-start.5 = (f32[128]{0:T(128)S(1)}, f32[128]{0:T(128)}, u32[]{:S(2)}) copy-start(f32[128]{0:T(128)} %param.19) | copy-start | bytes 1540
  9.1 22.4 %copy-start.6 = (s32[128]{0:T(128)S(1)}, s32[128]{0:T(128)}, u32[]{:S(2)}) copy-start(s32[128]{0:T(128)} %param.17) | copy-start | bytes 1540
  9.1 48.8 %copy-start.7 = (f32[128]{0:T(128)S(1)}, f32[128]{0:T(128)}, u32[]{:S(2)}) copy-start(f32[128]{0:T(128)} %param.18) | copy-start | bytes 1540
  9.1 48.8 %copy-start.8 = (s32[128]{0:T(128)S(1)}, s32[128]{0:T(128)}, u32[]{:S(2)}) copy-start(s32[128]{0:T(128)} %param.16) | copy-start | bytes 1540
  32.5 6.1 %collective-permute-start.2 = (f32[144,256]{1,0:T(8,128)S(1)}, f32[144,256]{1,0:T(8,128)S(1)}, u32[]{:S(2)}, u32[]{:S(2)}) collective-permute-start(f32[144,256]{1,0:T(8,128)S(1)} %get-tuple-element.37), channel_id=1, source_target_pairs={{0,1},{1,0},{2,3},{3,2},{4,5},{5,4},{6,7},{7,6},{8,10},{9,11},{10,... | collective-permute-start | bytes 442376 | tf_op jit(solution)/shard_map/ppermute | solution.py:781
  35.5 6.1 %collective-permute-start.3 = (f32[144,256]{1,0:T(8,128)S(1)}, f32[144,256]{1,0:T(8,128)S(1)}, u32[]{:S(2)}, u32[]{:S(2)}) collective-permute-start(f32[144,256]{1,0:T(8,128)S(1)} %get-tuple-element.38), channel_id=1, source_target_pairs={{0,2},{1,3},{2,0},{3,1},{4,6},{5,7},{6,4},{7,5},{8,9},{9,8},{10,11... | collective-permute-start | bytes 442376 | tf_op jit(solution)/shard_map/ppermute | solution.py:781
  37.1 7.8 %collective-permute-start.4 = (f32[144,256]{1,0:T(8,128)S(1)}, f32[144,256]{1,0:T(8,128)S(1)}, u32[]{:S(2)}, u32[]{:S(2)}) collective-permute-start(f32[144,256]{1,0:T(8,128)S(1)} %get-tuple-element.39), channel_id=1, source_target_pairs={{0,3},{1,2},{2,1},{3,0},{4,7},{5,6},{6,5},{7,4},{8,11},{9,10},{10,... | collective-permute-start | bytes 442376 | tf_op jit(solution)/shard_map/ppermute | solution.py:781
  45.8 7.5 %collective-permute-start.5 = (f32[88,256]{1,0:T(8,128)S(1)}, f32[88,256]{1,0:T(8,128)S(1)}, u32[]{:S(2)}, u32[]{:S(2)}) collective-permute-start(f32[88,256]{1,0:T(8,128)S(1)} %get-tuple-element.41.mine), channel_id=1, source_target_pairs={{0,4},{1,5},{2,6},{3,7},{4,0},{5,1},{6,2},{7,3},{8,12},{9,13},{10,... | collective-permute-start | bytes 270344 | tf_op jit(solution)/shard_map/ppermute | solution.py:773
  54.4 8.5 %collective-permute-start.6 = (f32[2,64,256]{2,1,0:T(8,128)S(1)}, f32[2,64,256]{2,1,0:T(8,128)S(1)}, u32[]{:S(2)}, u32[]{:S(2)}) collective-permute-start(f32[2,64,256]{2,1,0:T(8,128)S(1)} %get-tuple-element.48), channel_id=1, source_target_pairs={{0,1},{1,0},{2,3},{3,2},{4,5},{5,4},{6,7},{7,6},{8,10},{9,11},{10,... | collective-permute-start | bytes 393224 | tf_op jit(solution)/shard_map/ppermute | solution.py:781
  54.5 8.4 %collective-permute-start.7 = (f32[2,64,256]{2,1,0:T(8,128)S(1)}, f32[2,64,256]{2,1,0:T(8,128)S(1)}, u32[]{:S(2)}, u32[]{:S(2)}) collective-permute-start(f32[2,64,256]{2,1,0:T(8,128)S(1)} %get-tuple-element.49), channel_id=1, source_target_pairs={{0,2},{1,3},{2,0},{3,1},{4,6},{5,7},{6,4},{7,5},{8,9},{9,8},{10,11... | collective-permute-start | bytes 393224 | tf_op jit(solution)/shard_map/ppermute | solution.py:781
  55.1 7.8 %collective-permute-start.8 = (f32[2,64,256]{2,1,0:T(8,128)S(1)}, f32[2,64,256]{2,1,0:T(8,128)S(1)}, u32[]{:S(2)}, u32[]{:S(2)}) collective-permute-start(f32[2,64,256]{2,1,0:T(8,128)S(1)} %get-tuple-element.50), channel_id=1, source_target_pairs={{0,3},{1,2},{2,1},{3,0},{4,7},{5,6},{6,5},{7,4},{8,11},{9,10},{10,... | collective-permute-start | bytes 393224 | tf_op jit(solution)/shard_map/ppermute | solution.py:781

commit v4 on v3

--- a/solution.py
+++ b/solution.py
@@ -36,8 +36,12 @@
     return mask & ~3 | (mask & 1) << 1 | (mask & 2) >> 1
 
 
+def depth_of(where, count):
+    return where[0] & (count - 1)
+
+
 def partner(where, mask, blocks):
-    odd = where[1] & 1 if blocks >= 4 else 0
+    odd = where[0] // (2 * blocks) & 1 if blocks >= 4 else 0
     return (where[0] & (blocks - 1)) ^ (mask + odd * (crossed(mask) - mask))
 
 
@@ -259,7 +263,7 @@
     meta = 2 * lines
 
     entries = [table[k] for k in range(table.shape[0])]
-    level = lax.broadcasted_iota(jnp.int32, (slabs, wells), 0) + where_am_i[0] * slabs
+    level = lax.broadcasted_iota(jnp.int32, (slabs, wells), 0) + depth_of(where_am_i, 2 * copies) * slabs
     rock = cells[0]
     cond = select_tree(cells[1].astype(jnp.int32), entries)
     rate = jnp.where(level < reach[...], speed[...] * cond / (1.0 + cond), 0.0)
@@ -417,7 +421,7 @@
     lines = (rows - META_ROWS) // 2
     for m, piece in enumerate(piece_refs):
         fl_ref[partner(where, m, blocks)] = piece[...]
-    flip = where[0] // blocks
+    flip = depth_of(where, 2 * blocks) // blocks
     flipped = flip == 1
     block = [k + flip * (blocks - 1 - 2 * k) for k in range(blocks)]
     entries, _ = half_chain(
@@ -476,7 +480,7 @@
 def second_kernel(slabs, where, fl_ref, mine, other, *refs):
     out_refs, (info_ref, table, uv_ref) = refs[:-3], refs[-3:]
     blocks, _, lines, share = uv_ref.shape
-    flip = where[0] // blocks
+    flip = depth_of(where, 2 * blocks) // blocks
     flipped = flip == 1
     block = [k + flip * (blocks - 1 - 2 * k) for k in range(blocks)]
     for j in range(blocks):
@@ -544,7 +548,7 @@
 def extras_kernel(where_am_i, info, source, flux, inverse, inlet, holders, wells_ref, rows_ref, leaving, found):
     blocks = info.shape[0]
     slabs, wells = wells_ref.shape
-    d = where_am_i[0]
+    d = depth_of(where_am_i, blocks)
     dot = functools.partial(jnp.dot, precision=HIGHEST, preferred_element_type=jnp.float32)
     row_of = lambda j, n: info[j, 2 + n : 3 + n, :wells]
     down, rise = [None] * blocks, [None] * blocks
@@ -745,7 +749,7 @@
     parts = depth_count // 2
 
     place_row = well_position_inside.reshape(1, wells)
-    where = jnp.stack([depth_index, lax.axis_index("strip")])
+    where = lax.axis_index(("strip", "depth")).reshape(1)
     first, last = edge_rows(warmth_before, stratum_category, table)
     first, last, place_row, where = lax.optimization_barrier((first, last, place_row, where))
     count = lax.axis_size("strip")

time: 70.7 us -> 69 us (0.976)
  Pallas kernels: 37.8 us -> 35.6 us
where the time goes in v4:
time: 69 us; the launch traced here: 68.8 us
  Pallas kernels  35.6 us (52%)
  waiting for transfers between devices  16.4 us (24%)
  starting transfers between devices  15.2 us (22%)
  between operations  1.49 us (2%)
    pallas_call x1, Pallas kernels, stencil(): pl.pallas_call(stencil_kernel, grid=(slabs // planes,), in_specs=[smem, s...  22.3 us
    ppermute x6, waiting for transfers between devices, with_partner(): return lax.ppermute(value, ('strip', 'depth'), perm)  11.7 us
    ppermute x6, starting transfers between devices, with_partner(): return lax.ppermute(value, ('strip', 'depth'), perm)  8.13 us
    pallas_call x1, Pallas kernels, solve(): pl.pallas_call(solve_kernel, grid=(groups // together,), in_specs=[pl.Blo...  7.18 us
    ppermute x1, waiting for transfers between devices, swapped(): lax.ppermute(value, 'depth', [(i, i ^ mask) for i in range(depth_count)])  4.75 us
    pallas_call x1, Pallas kernels, edge_rows(): pl.pallas_call(edge_kernel, grid=(1,), in_specs=[pl.BlockSpec(memory_spac...  3.32 us
    ppermute x1, starting transfers between devices, body(): before = lax.ppermute(last, 'strip', up)  3.05 us
    ppermute x1, starting transfers between devices, swapped(): lax.ppermute(value, 'depth', [(i, i ^ mask) for i in range(depth_count)])  2.79 us
  transfers between devices with their start and end apart: 9, of which 5 were waited for; matrix products, arithmetic and copies ran while one was open for 0% of the time, Pallas kernels for 34%

profile of v4, /device:TPU:0, one launch (start us, length us, event | category | flops | bytes accessed | tf_op | source)
XLA Modules:
  0.0 68.8 jit_solution(8740967726300657983)
XLA Ops:
  0.6 0.0 copy-start.2
  0.6 0.0 copy-start.3
  0.7 0.0 copy-start.4
  0.7 3.3 %edge_rows.1 = (f32[2,32,1024]{2,1,0:T(8,128)}, f32[2,32,1024]{2,1,0:T(8,128)}) custom-call(f32[8]{0:T(128)} %table.5, f32[32,64,1024]{2,1,0:T(8,128)} %w_ref.1, s32[32,64,1024]{2,1,0:T(8,128)} %cat_ref.1, f32[32,64,1024]{2,1,0:T(8,128)} %w_ref.1, s32[32,64,1024]{2,1,0:T(8,128)} %cat_ref.1), custom_call_target="tpu_custom_call" | custom-call | flops 1000000 | bytes 2097152 | tf_op jit(solution)/shard_map/edge_rows/pallas_call | solution.py:80
  4.0 1.3 %collective-permute-start.1 = (f32[2,32,1024]{2,1,0:T(8,128)}, f32[2,32,1024]{2,1,0:T(8,128)S(1)}, u32[]{:S(2)}, u32[]{:S(2)}) collective-permute-start(f32[2,32,1024]{2,1,0:T(8,128)} %get-tuple-element.33.first), channel_id=1, source_target_pairs={{8,0},{16,8},{24,16},{9,1},{17,9},{25,17},{10,2},{18,10},{26,18},{... | collective-permute-start | bytes 786440 | tf_op jit(solution)/shard_map/ppermute | solution.py:759
  5.3 3.0 %collective-permute-start = (f32[2,32,1024]{2,1,0:T(8,128)}, f32[2,32,1024]{2,1,0:T(8,128)S(1)}, u32[]{:S(2)}, u32[]{:S(2)}) collective-permute-start(f32[2,32,1024]{2,1,0:T(8,128)} %get-tuple-element.34.last), channel_id=1, source_target_pairs={{0,8},{8,16},{16,24},{1,9},{9,17},{17,25},{2,10},{10,18},{18,26},{... | collective-permute-start | bytes 786440 | tf_op jit(solution)/shard_map/ppermute | solution.py:758
  9.0 0.0 copy-done.2
  9.0 0.0 copy-done.3
  9.0 0.0 copy-done.4
  9.0 0.0 copy-start
  9.0 0.0 copy-start.1
  9.0 0.0 copy-start.5
  9.0 0.0 copy-start.6
  9.1 0.0 copy-start.7
  9.1 0.0 copy-start.8
  9.1 22.3 %stencil.1 = (f32[8,32,8,1024]{3,2,1,0:T(8,128)S(1)}, f32[2,64,1024]{2,1,0:T(8,128)S(1)}, f32[2,32,128]{2,1,0:T(8,128)S(1)}) custom-call(f32[8]{0:T(128)S(1)} %copy-done.3, f32[32,32]{1,0:T(8,128)S(1)} %copy-done.2, f32[32,64,1024]{2,1,0:T(8,128)} %w_ref.1, s32[32,64,1024]{2,1,0:T(8,128)} %cat_ref.1, s32[1,128]{1,0:T(1,128)S(1)} %bitcast.7), custom_call_target="tpu_custom_call" | custom-call | flops 83886080 | bytes 25165824 | tf_op jit(solution)/shard_map/stencil/pallas_call | solution.py:207
  31.3 0.0 collective-permute-done.1.after
  31.4 0.0 collective-permute-done.before
  31.4 0.0 copy-done
  31.4 0.0 copy-done.1
  31.4 0.0 copy-done.5
  31.4 0.0 copy-done.6
  31.4 1.0 %payload.1 = (f32[144,256]{1,0:T(8,128)S(1)}, f32[144,256]{1,0:T(8,128)S(1)}, f32[144,256]{1,0:T(8,128)S(1)}, f32[144,256]{1,0:T(8,128)S(1)}, f32[2,32,1024]{2,1,0:T(8,128)S(1)}, /*index=5*/f32[3,32,128]{2,1,0:T(8,128)S(1)}) custom-call(f32[1]{0:T(128)S(6)} %copy.12.ratio, f32[8]{0:T(128)S(1)} %copy-done.3, s32[1]{0:T(128)} %bitcast.1.where_am_i.where, ...), custom_call_target="tpu_custom_call" | custom-call | flops 1000000 | bytes 1000000 | tf_op jit(solution)/shard_map/payload/pallas_call | solution.py:315
  32.5 3.0 %collective-permute-start.2 = (f32[144,256]{1,0:T(8,128)S(1)}, f32[144,256]{1,0:T(8,128)S(1)}, u32[]{:S(2)}, u32[]{:S(2)}) collective-permute-start(f32[144,256]{1,0:T(8,128)S(1)} %get-tuple-element.37), channel_id=1, source_target_pairs={{0,1},{1,0},{2,3},{3,2},{4,5},{5,4},{6,7},{7,6},{8,10},{9,11},{10,... | collective-permute-start | bytes 442376 | tf_op jit(solution)/shard_map/ppermute | solution.py:785
  35.5 1.6 %collective-permute-start.3 = (f32[144,256]{1,0:T(8,128)S(1)}, f32[144,256]{1,0:T(8,128)S(1)}, u32[]{:S(2)}, u32[]{:S(2)}) collective-permute-start(f32[144,256]{1,0:T(8,128)S(1)} %get-tuple-element.38), channel_id=1, source_target_pairs={{0,2},{1,3},{2,0},{3,1},{4,6},{5,7},{6,4},{7,5},{8,9},{9,8},{10,11... | collective-permute-start | bytes 442376 | tf_op jit(solution)/shard_map/ppermute | solution.py:785
  37.0 0.0 collective-permute-start.4
  37.0 1.5 %collective-permute-done.2.refs_1_ = f32[144,256]{1,0:T(8,128)S(1)} collective-permute-done((f32[144,256]{1,0:T(8,128)S(1)}, f32[144,256]{1,0:T(8,128)S(1)}, u32[]{:S(2)}, u32[]{:S(2)}) %collective-permute-start.2) | collective-permute-done | bytes 147488 | tf_op jit(solution)/shard_map/ppermute | solution.py:785
  38.6 2.9 %collective-permute-done.3.refs_2_ = f32[144,256]{1,0:T(8,128)S(1)} collective-permute-done((f32[144,256]{1,0:T(8,128)S(1)}, f32[144,256]{1,0:T(8,128)S(1)}, u32[]{:S(2)}, u32[]{:S(2)}) %collective-permute-start.3) | collective-permute-done | bytes 147488 | tf_op jit(solution)/shard_map/ppermute | solution.py:785
  41.5 3.3 %collective-permute-done.4.refs_3_ = f32[144,256]{1,0:T(8,128)S(1)} collective-permute-done((f32[144,256]{1,0:T(8,128)S(1)}, f32[144,256]{1,0:T(8,128)S(1)}, u32[]{:S(2)}, u32[]{:S(2)}) %collective-permute-start.4) | collective-permute-done | bytes 147488 | tf_op jit(solution)/shard_map/ppermute | solution.py:785
  44.8 0.3 reduced_in.1
  45.1 2.8 %collective-permute-start.5 = (f32[88,256]{1,0:T(8,128)S(1)}, f32[88,256]{1,0:T(8,128)S(1)}, u32[]{:S(2)}, u32[]{:S(2)}) collective-permute-start(f32[88,256]{1,0:T(8,128)S(1)} %get-tuple-element.41.mine), channel_id=1, source_target_pairs={{0,4},{1,5},{2,6},{3,7},{4,0},{5,1},{6,2},{7,3},{8,12},{9,13},{10,... | collective-permute-start | bytes 270344 | tf_op jit(solution)/shard_map/ppermute | solution.py:777
  47.9 4.7 %collective-permute-done.5.other = f32[88,256]{1,0:T(8,128)S(1)} collective-permute-done((f32[88,256]{1,0:T(8,128)S(1)}, f32[88,256]{1,0:T(8,128)S(1)}, u32[]{:S(2)}, u32[]{:S(2)}) %collective-permute-start.5) | collective-permute-done | bytes 90144 | tf_op jit(solution)/shard_map/ppermute | solution.py:777
  52.7 0.5 reduced_out.1
  53.2 0.1 collective-permute-start.6
  53.3 0.6 collective-permute-start.7
  53.9 2.9 %collective-permute-start.8 = (f32[2,64,256]{2,1,0:T(8,128)S(1)}, f32[2,64,256]{2,1,0:T(8,128)S(1)}, u32[]{:S(2)}, u32[]{:S(2)}) collective-permute-start(f32[2,64,256]{2,1,0:T(8,128)S(1)} %get-tuple-element.50), channel_id=1, source_target_pairs={{0,3},{1,2},{2,1},{3,0},{4,7},{5,6},{6,5},{7,4},{8,11},{9,10},{10,... | collective-permute-start | bytes 393224 | tf_op jit(solution)/shard_map/ppermute | solution.py:785
  56.8 0.0 copy-done.7
  56.8 0.0 copy-done.8
  56.8 1.0 %extras.1 = (f32[32,128]{1,0:T(8,128)S(1)}, f32[2,32,1024]{2,1,0:T(8,128)S(1)}, f32[1,16]{1,0:T(1,128)}) custom-call(s32[1]{0:T(128)} %bitcast.1.where_am_i.where, f32[8,16,128]{2,1,0:T(8,128)S(1)} %get-tuple-element.42.info, f32[3,32,128]{2,1,0:T(8,128)S(1)} %get-tuple-element.43.source, f32[2,32,1024]{2,1,0:T(8,128)S(1)} %get-tuple-element.44.flux, ...), custom_call_target="tpu_custom_call" | custom-call | flops 10000000 | bytes 1000000 | tf_op jit(solution)/shard_map/extras/pallas_call | solution.py:601
  57.7 3.9 %collective-permute-done.6.refs_1_ = f32[2,64,256]{2,1,0:T(8,128)S(1)} collective-permute-done((f32[2,64,256]{2,1,0:T(8,128)S(1)}, f32[2,64,256]{2,1,0:T(8,128)S(1)}, u32[]{:S(2)}, u32[]{:S(2)}) %collective-permute-start.6) | collective-permute-done | bytes 131104 | tf_op jit(solution)/shard_map/ppermute | solution.py:785
  61.6 0.0 collective-permute-done.7.refs_2_
  61.6 0.0 collective-permute-done.8.refs_3_
  61.7 7.2 %depth_solve.1 = f32[32,64,1024]{2,1,0:T(8,128)} custom-call(s32[1]{0:T(128)} %bitcast.1.where_am_i.where, f32[8,32,8,1024]{3,2,1,0:T(8,128)S(1)} %get-tuple-element.31.right, f32[32,32]{1,0:T(8,128)S(1)} %copy-done.2, s32[1,128]{1,0:T(1,128)S(1)} %bitcast.8, f32[32,128]{1,0:T(8,128)S(1)} %get-tuple-element.45.solved_wells, ...), custom_call_target="tpu_custom_call" | custom-call | flops 4294967296 | bytes 16777216 | tf_op jit(solution)/shard_map/depth_solve/pallas_call | solution.py:703
Async XLA Ops:
  0.6 8.3 %copy-start.2 = (f32[32,32]{1,0:T(8,128)S(1)}, f32[32,32]{1,0:T(8,128)}, u32[]{:S(2)}) copy-start(f32[32,32]{1,0:T(8,128)} %inverse.5) | copy-start | bytes 12292
  0.6 8.3 %copy-start.3 = (f32[8]{0:T(128)S(1)}, f32[8]{0:T(128)}, u32[]{:S(2)}) copy-start(f32[8]{0:T(128)} %table.5) | copy-start | bytes 100
  0.7 8.3 %copy-start.4 = (s32[128]{0:T(128)S(1)}, s32[128]{0:T(128)}, u32[]{:S(2)}) copy-start(s32[128]{0:T(128)} %param.15) | copy-start | bytes 1540
  4.0 27.4 %collective-permute-start.1 = (f32[2,32,1024]{2,1,0:T(8,128)}, f32[2,32,1024]{2,1,0:T(8,128)S(1)}, u32[]{:S(2)}, u32[]{:S(2)}) collective-permute-start(f32[2,32,1024]{2,1,0:T(8,128)} %get-tuple-element.33.first), channel_id=1, source_target_pairs={{8,0},{16,8},{24,16},{9,1},{17,9},{25,17},{10,2},{18,10},{26,18},{... | collective-permute-start | bytes 786440 | tf_op jit(solution)/shard_map/ppermute | solution.py:759
  5.3 26.1 %collective-permute-start = (f32[2,32,1024]{2,1,0:T(8,128)}, f32[2,32,1024]{2,1,0:T(8,128)S(1)}, u32[]{:S(2)}, u32[]{:S(2)}) collective-permute-start(f32[2,32,1024]{2,1,0:T(8,128)} %get-tuple-element.34.last), channel_id=1, source_target_pairs={{0,8},{8,16},{16,24},{1,9},{9,17},{17,25},{2,10},{10,18},{18,26},{... | collective-permute-start | bytes 786440 | tf_op jit(solution)/shard_map/ppermute | solution.py:758
  9.0 22.4 %copy-start = (f32[2,32,1024]{2,1,0:T(8,128)S(1)}, f32[2,32,1024]{2,1,0:T(8,128)}, u32[]{:S(2)}) copy-start(f32[2,32,1024]{2,1,0:T(8,128)} %get-tuple-element.33.first) | copy-start | bytes 786436
  9.0 22.4 %copy-start.1 = (f32[2,32,1024]{2,1,0:T(8,128)S(1)}, f32[2,32,1024]{2,1,0:T(8,128)}, u32[]{:S(2)}) copy-start(f32[2,32,1024]{2,1,0:T(8,128)} %get-tuple-element.34.last) | copy-start | bytes 786436
  9.0 22.4 %copy-start.5 = (f32[128]{0:T(128)S(1)}, f32[128]{0:T(128)}, u32[]{:S(2)}) copy-start(f32[128]{0:T(128)} %param.19) | copy-start | bytes 1540
  9.0 22.4 %copy-start.6 = (s32[128]{0:T(128)S(1)}, s32[128]{0:T(128)}, u32[]{:S(2)}) copy-start(s32[128]{0:T(128)} %param.17) | copy-start | bytes 1540
  9.1 47.7 %copy-start.7 = (f32[128]{0:T(128)S(1)}, f32[128]{0:T(128)}, u32[]{:S(2)}) copy-start(f32[128]{0:T(128)} %param.18) | copy-start | bytes 1540
  9.1 47.7 %copy-start.8 = (s32[128]{0:T(128)S(1)}, s32[128]{0:T(128)}, u32[]{:S(2)}) copy-start(s32[128]{0:T(128)} %param.16) | copy-start | bytes 1540
  32.5 6.1 %collective-permute-start.2 = (f32[144,256]{1,0:T(8,128)S(1)}, f32[144,256]{1,0:T(8,128)S(1)}, u32[]{:S(2)}, u32[]{:S(2)}) collective-permute-start(f32[144,256]{1,0:T(8,128)S(1)} %get-tuple-element.37), channel_id=1, source_target_pairs={{0,1},{1,0},{2,3},{3,2},{4,5},{5,4},{6,7},{7,6},{8,10},{9,11},{10,... | collective-permute-start | bytes 442376 | tf_op jit(solution)/shard_map/ppermute | solution.py:785
  35.5 6.0 %collective-permute-start.3 = (f32[144,256]{1,0:T(8,128)S(1)}, f32[144,256]{1,0:T(8,128)S(1)}, u32[]{:S(2)}, u32[]{:S(2)}) collective-permute-start(f32[144,256]{1,0:T(8,128)S(1)} %get-tuple-element.38), channel_id=1, source_target_pairs={{0,2},{1,3},{2,0},{3,1},{4,6},{5,7},{6,4},{7,5},{8,9},{9,8},{10,11... | collective-permute-start | bytes 442376 | tf_op jit(solution)/shard_map/ppermute | solution.py:785
  37.0 7.8 %collective-permute-start.4 = (f32[144,256]{1,0:T(8,128)S(1)}, f32[144,256]{1,0:T(8,128)S(1)}, u32[]{:S(2)}, u32[]{:S(2)}) collective-permute-start(f32[144,256]{1,0:T(8,128)S(1)} %get-tuple-element.39), channel_id=1, source_target_pairs={{0,3},{1,2},{2,1},{3,0},{4,7},{5,6},{6,5},{7,4},{8,11},{9,10},{10,... | collective-permute-start | bytes 442376 | tf_op jit(solution)/shard_map/ppermute | solution.py:785
  45.1 7.5 %collective-permute-start.5 = (f32[88,256]{1,0:T(8,128)S(1)}, f32[88,256]{1,0:T(8,128)S(1)}, u32[]{:S(2)}, u32[]{:S(2)}) collective-permute-start(f32[88,256]{1,0:T(8,128)S(1)} %get-tuple-element.41.mine), channel_id=1, source_target_pairs={{0,4},{1,5},{2,6},{3,7},{4,0},{5,1},{6,2},{7,3},{8,12},{9,13},{10,... | collective-permute-start | bytes 270344 | tf_op jit(solution)/shard_map/ppermute | solution.py:777
  53.2 8.4 %collective-permute-start.6 = (f32[2,64,256]{2,1,0:T(8,128)S(1)}, f32[2,64,256]{2,1,0:T(8,128)S(1)}, u32[]{:S(2)}, u32[]{:S(2)}) collective-permute-start(f32[2,64,256]{2,1,0:T(8,128)S(1)} %get-tuple-element.48), channel_id=1, source_target_pairs={{0,1},{1,0},{2,3},{3,2},{4,5},{5,4},{6,7},{7,6},{8,10},{9,11},{10,... | collective-permute-start | bytes 393224 | tf_op jit(solution)/shard_map/ppermute | solution.py:785
  53.3 8.4 %collective-permute-start.7 = (f32[2,64,256]{2,1,0:T(8,128)S(1)}, f32[2,64,256]{2,1,0:T(8,128)S(1)}, u32[]{:S(2)}, u32[]{:S(2)}) collective-permute-start(f32[2,64,256]{2,1,0:T(8,128)S(1)} %get-tuple-element.49), channel_id=1, source_target_pairs={{0,2},{1,3},{2,0},{3,1},{4,6},{5,7},{6,4},{7,5},{8,9},{9,8},{10,11... | collective-permute-start | bytes 393224 | tf_op jit(solution)/shard_map/ppermute | solution.py:785
  53.9 7.8 %collective-permute-start.8 = (f32[2,64,256]{2,1,0:T(8,128)S(1)}, f32[2,64,256]{2,1,0:T(8,128)S(1)}, u32[]{:S(2)}, u32[]{:S(2)}) collective-permute-start(f32[2,64,256]{2,1,0:T(8,128)S(1)} %get-tuple-element.50), channel_id=1, source_target_pairs={{0,3},{1,2},{2,1},{3,0},{4,7},{5,6},{6,5},{7,4},{8,11},{9,10},{10,... | collective-permute-start | bytes 393224 | tf_op jit(solution)/shard_map/ppermute | solution.py:785
